TPU v7x, 128 devices: a whole 4x4x4 slice. The times are simulated.
128 devices in a mesh: section: 2 (over y_hi), fsdp: 64 (over x, y_lo, z, core).
Axes of the slice: x: 4, y: 4 (y_hi: 2, y_lo: 2; y = y_hi * 2 + y_lo), z: 4, core: 2. Of those that a mesh axis runs over, the one named last changes fastest.
Arguments:
- tokens_in: bfloat16 [2, 64, 128, 896], P(None, 'fsdp'), may hold values from -6 to 6
- out_grad: bfloat16 [2, 64, 128, 896], P(None, 'fsdp'), may hold values from -6 to 6
- segments: int32 [2, 64, 128], P(None, 'fsdp'), may hold values from 0 to 3, never falling along the last dimension, each value on 1 to 64 neighbouring positions
- norm1_gain: bfloat16 [2, 896], P('section', 'fsdp'), may hold values from 0.099609375 to 1.8984375
- qkv_weight: bfloat16 [2, 896, 1152], P('section', 'fsdp'), may hold values from -0.1875 to 0.1875
- qkv_bias: bfloat16 [2, 1152], P('section', 'fsdp'), may hold values from -3 to 3
- out_weight: bfloat16 [2, 896, 896], P('section', 'fsdp'), may hold values from -0.75 to 0.75
- norm2_gain: bfloat16 [2, 896], P('section', 'fsdp'), may hold values from 0.099609375 to 1.8984375
- gate_weight: bfloat16 [2, 896, 4864], P('section', 'fsdp'), may hold values from -0.1875 to 0.1875
- up_weight: bfloat16 [2, 896, 4864], P('section', 'fsdp'), may hold values from -0.1875 to 0.1875
- down_weight: bfloat16 [2, 4864, 896], P('section', 'fsdp'), may hold values from -0.078125 to 0.078125
Outputs:
- section_out: bfloat16 [2, 2, 64, 128, 896], P('section', None, 'fsdp')
- section_in_grad: bfloat16 [2, 2, 64, 128, 896], P('section', None, 'fsdp')
- norm1_gain_grad: float32 [2, 896], P('section', 'fsdp')
- qkv_weight_grad: float32 [2, 896, 1152], P('section', 'fsdp')
- qkv_bias_grad: float32 [2, 1152], P('section', 'fsdp')
- out_weight_grad: float32 [2, 896, 896], P('section', 'fsdp')
- norm2_gain_grad: float32 [2, 896], P('section', 'fsdp')
- gate_weight_grad: float32 [2, 896, 4864], P('section', 'fsdp')
- up_weight_grad: float32 [2, 896, 4864], P('section', 'fsdp')
- down_weight_grad: float32 [2, 4864, 896], P('section', 'fsdp')
Inputs may be any that keep to these rules, and one draw needn't show every extreme that they name: `segments`: along each sequence the segment numbers never fall; a document covers at most 64 tokens of its sequence, and some document covers exactly that many.
All inputs are finite; a program needn't handle non-finite values.
Results may differ from a plain program's by a relative error of at most 0.023.
Values may be sent and summed in bfloat16 or wider, within the bound.
A program may use at most 192 MiB of HBM per device.

v0:
```python
import math

import jax
import jax.numpy as jnp
from jax import lax
from jax.sharding import PartitionSpec as P

HEADS = 14
KV_HEADS = 2
HEAD_DIM = 64


norm_epsilon = 1e-06
rope_base = 1000000.0


def passed_along(block, axis, distance):
    devices = range(lax.axis_size(axis))
    route = [(i - distance, i) for i in devices if i - distance in devices]
    return lax.ppermute(block, axis, route)


def rope_tables(segment_row, head_size):
    length = segment_row.shape[0]
    places = jnp.arange(length, dtype=jnp.int32)
    changes = jnp.concatenate(
        [jnp.ones((1,), jnp.int32), (segment_row[1:] != segment_row[:-1]).astype(jnp.int32)]
    )
    starts = lax.cummax(places * changes, axis=0)
    offsets = (places - starts).astype(jnp.float32)
    ladder = jnp.arange(head_size // 2, dtype=jnp.float32) * (
        -2.0 * math.log(rope_base) / head_size
    )
    angles = offsets[:, None] * jnp.exp(ladder)[None, :]
    angles = jnp.concatenate([angles, angles], axis=-1)
    return (jnp.cos(angles), jnp.sin(angles))


def rotate_half(head_block):
    half_width = head_block.shape[-1] // 2
    return jnp.concatenate([-head_block[..., half_width:], head_block[..., :half_width]], axis=-1)


def spin(head_block, cosine_table, sine_table):
    return head_block * cosine_table + rotate_half(head_block) * sine_table


def spin_back(grad_rotated, cosine_table, sine_table):
    return grad_rotated * cosine_table - rotate_half(grad_rotated * sine_table)


def visible(segment_row):
    places = jnp.arange(segment_row.shape[0], dtype=jnp.int32)
    return (segment_row[:, None] == segment_row[None, :]) & (places[None, :] <= places[:, None])


def score_block(query_low, key_low, allowed):
    scores = jnp.einsum(
        "qkgd,skd->kgqs", query_low, key_low, preferred_element_type=jnp.float32
    ) * HEAD_DIM ** (-0.5)
    return jnp.where(allowed[None, None], scores, -1e30)


def layer_forward(stream, weights, segment_row):
    gain_one, w_qkv, b_qkv, w_out, gain_two, w_gate, w_up, w_down = weights
    length, model_width = stream.shape
    pair_width = KV_HEADS * HEAD_DIM
    groups = HEADS // KV_HEADS
    cosine_table, sine_table = rope_tables(segment_row, HEAD_DIM)
    scale_one = lax.rsqrt(jnp.mean(stream * stream, axis=-1, keepdims=True) + norm_epsilon)
    normed_one = (stream * scale_one * gain_one.astype(jnp.float32)).astype(jnp.bfloat16)
    mixed_qkv = jnp.dot(normed_one, w_qkv, preferred_element_type=jnp.float32) + b_qkv.astype(
        jnp.float32
    )
    queries = spin(
        mixed_qkv[:, :model_width].reshape(length, HEADS, HEAD_DIM),
        cosine_table[:, None, :],
        sine_table[:, None, :],
    )
    key_rows = spin(
        mixed_qkv[:, model_width : model_width + pair_width].reshape(length, KV_HEADS, HEAD_DIM),
        cosine_table[:, None, :],
        sine_table[:, None, :],
    )
    value_rows = mixed_qkv[:, model_width + pair_width :].reshape(length, KV_HEADS, HEAD_DIM)
    query_low = queries.astype(jnp.bfloat16).reshape(length, KV_HEADS, groups, HEAD_DIM)
    key_low = key_rows.astype(jnp.bfloat16)
    value_low = value_rows.astype(jnp.bfloat16)
    scores = score_block(query_low, key_low, visible(segment_row))
    row_max = jnp.max(scores, axis=-1, keepdims=True)
    exponent = jnp.exp(scores - row_max)
    row_total = jnp.sum(exponent, axis=-1, keepdims=True)
    attn_probs = (exponent / row_total).astype(jnp.bfloat16)
    log_norm = (row_max + jnp.log(row_total))[..., 0]
    attended = jnp.einsum(
        "kgqs,skd->qkgd", attn_probs, value_low, preferred_element_type=jnp.float32
    )
    attended = attended.reshape(length, model_width).astype(jnp.bfloat16)
    middle = stream + jnp.dot(attended, w_out, preferred_element_type=jnp.float32)
    scale_two = lax.rsqrt(jnp.mean(middle * middle, axis=-1, keepdims=True) + norm_epsilon)
    normed_two = (middle * scale_two * gain_two.astype(jnp.float32)).astype(jnp.bfloat16)
    gate_value = jnp.dot(normed_two, w_gate, preferred_element_type=jnp.float32)
    up_value = jnp.dot(normed_two, w_up, preferred_element_type=jnp.float32)
    hidden = (jax.nn.silu(gate_value) * up_value).astype(jnp.bfloat16)
    result = middle + jnp.dot(hidden, w_down, preferred_element_type=jnp.float32)
    kept_values = (
        stream,
        scale_one,
        normed_one,
        query_low,
        key_low,
        value_low,
        log_norm,
        attended,
        middle,
        scale_two,
        normed_two,
        gate_value,
        up_value,
        hidden,
    )
    return (result, kept_values)


def layer_backward(grad_out, kept_values, weights, segment_row):
    (
        stream,
        scale_one,
        normed_one,
        query_low,
        key_low,
        value_low,
        log_norm,
        attended,
        middle,
        scale_two,
        normed_two,
        gate_value,
        up_value,
        hidden,
    ) = kept_values
    gain_one, w_qkv, b_qkv, w_out, gain_two, w_gate, w_up, w_down = weights
    length, model_width = stream.shape
    groups = HEADS // KV_HEADS
    score_scale = HEAD_DIM ** (-0.5)
    cosine_table, sine_table = rope_tables(segment_row, HEAD_DIM)
    grad_hidden = jnp.einsum("rd,fd->rf", grad_out, w_down, preferred_element_type=jnp.float32)
    sigmoid_gate = jax.nn.sigmoid(gate_value)
    grad_gate = (
        grad_hidden * up_value * sigmoid_gate * (1.0 + gate_value * (1.0 - sigmoid_gate))
    ).astype(jnp.bfloat16)
    grad_up = (grad_hidden * gate_value * sigmoid_gate).astype(jnp.bfloat16)
    grad_normed_two = jnp.einsum("rf,df->rd", grad_gate, w_gate, preferred_element_type=jnp.float32)
    grad_normed_two = grad_normed_two + jnp.einsum(
        "rf,df->rd", grad_up, w_up, preferred_element_type=jnp.float32
    )
    grad_gain_two = jnp.sum(grad_normed_two * middle * scale_two, axis=0)
    scaled_two = grad_normed_two * gain_two.astype(jnp.float32)
    grad_middle = (
        grad_out.astype(jnp.float32)
        + scale_two * scaled_two
        - middle * scale_two**3 * jnp.mean(scaled_two * middle, axis=-1, keepdims=True)
    )
    grad_branch = grad_middle.astype(jnp.bfloat16)
    grad_attended = jnp.einsum(
        "rd,ed->re", grad_branch, w_out, preferred_element_type=jnp.float32
    ).astype(jnp.bfloat16)
    allowed = visible(segment_row)
    scores = score_block(query_low, key_low, allowed)
    attn_full = jnp.where(allowed[None, None], jnp.exp(scores - log_norm[..., None]), 0.0)
    attn_probs = attn_full.astype(jnp.bfloat16)
    grad_context = grad_attended.reshape(length, KV_HEADS, groups, HEAD_DIM)
    grad_values = jnp.einsum(
        "kgqs,qkgd->skd", attn_probs, grad_context, preferred_element_type=jnp.float32
    )
    grad_probs = jnp.einsum(
        "qkgd,skd->kgqs", grad_context, value_low, preferred_element_type=jnp.float32
    )
    grad_scores = (
        attn_full * (grad_probs - jnp.sum(attn_full * grad_probs, axis=-1, keepdims=True))
    ).astype(jnp.bfloat16)
    grad_queries = (
        jnp.einsum("kgqs,skd->qkgd", grad_scores, key_low, preferred_element_type=jnp.float32)
        * score_scale
    )
    grad_keys = (
        jnp.einsum("kgqs,qkgd->skd", grad_scores, query_low, preferred_element_type=jnp.float32)
        * score_scale
    )
    grad_queries = spin_back(
        grad_queries.reshape(length, HEADS, HEAD_DIM),
        cosine_table[:, None, :],
        sine_table[:, None, :],
    )
    grad_keys = spin_back(grad_keys, cosine_table[:, None, :], sine_table[:, None, :])
    grad_mixed = jnp.concatenate(
        [
            grad_queries.reshape(length, -1),
            grad_keys.reshape(length, -1),
            grad_values.reshape(length, -1),
        ],
        axis=1,
    ).astype(jnp.bfloat16)
    grad_bias = jnp.sum(grad_mixed, axis=0, dtype=jnp.float32)
    grad_normed_one = jnp.einsum("rc,dc->rd", grad_mixed, w_qkv, preferred_element_type=jnp.float32)
    grad_gain_one = jnp.sum(grad_normed_one * stream * scale_one, axis=0)
    scaled_one = grad_normed_one * gain_one.astype(jnp.float32)
    grad_stream = (
        grad_middle
        + scale_one * scaled_one
        - stream * scale_one**3 * jnp.mean(scaled_one * stream, axis=-1, keepdims=True)
    )
    operand_pairs = (
        (normed_one, grad_mixed),
        (attended, grad_branch),
        (normed_two, grad_gate),
        (normed_two, grad_up),
        (hidden, grad_out),
    )
    return (grad_stream, (grad_gain_one, grad_bias, grad_gain_two), operand_pairs)


def weight_pass(operand_pairs):
    return tuple(
        (
            jnp.einsum("ra,rb->ab", left_rows, right_rows, preferred_element_type=jnp.float32)
            for left_rows, right_rows in operand_pairs
        )
    )


def skipped(function):

    def silent(*operands):
        return jax.tree.map(jnp.zeros_like, function(*operands))

    return silent


def shards(
    tokens_in,
    out_grad,
    segments,
    norm1_gain,
    qkv_weight,
    qkv_bias,
    out_weight,
    norm2_gain,
    gate_weight,
    up_weight,
    down_weight,
):
    section_index = lax.axis_index("section")
    micro_count = tokens_in.shape[0]
    seq_length = tokens_in.shape[2]
    model_width = tokens_in.shape[3]
    segment_rows = segments[:, 0]
    gathered = (
        lax.all_gather(norm1_gain[0], "fsdp", axis=0, tiled=True),
        lax.all_gather(qkv_weight[0], "fsdp", axis=0, tiled=True),
        lax.all_gather(qkv_bias[0], "fsdp", axis=0, tiled=True),
        lax.all_gather(out_weight[0], "fsdp", axis=0, tiled=True),
        lax.all_gather(norm2_gain[0], "fsdp", axis=0, tiled=True),
        lax.all_gather(gate_weight[0], "fsdp", axis=0, tiled=True),
        lax.all_gather(up_weight[0], "fsdp", axis=0, tiled=True),
        lax.all_gather(down_weight[0], "fsdp", axis=0, tiled=True),
    )

    def run_forward(source, segment_row):
        return layer_forward(source, gathered, segment_row)

    arrived = jnp.zeros((seq_length, model_width), jnp.bfloat16)
    section_rows = []
    kept_rows = []
    for tick_step in range(micro_count + 1):
        micro_index = tick_step - section_index
        in_range = (micro_index >= 0) & (micro_index < micro_count)
        picked = jnp.clip(micro_index, 0, micro_count - 1)
        fresh_rows = tokens_in[min(tick_step, micro_count - 1), 0]
        source = jnp.where(section_index == 0, fresh_rows, arrived).astype(jnp.float32)
        segment_row = lax.dynamic_index_in_dim(segment_rows, picked, 0, keepdims=False)
        result, kept_values = lax.cond(
            in_range, run_forward, skipped(run_forward), source, segment_row
        )
        outgoing = result.astype(jnp.bfloat16)
        section_rows.append(outgoing)
        kept_rows.append(kept_values)
        if tick_step < micro_count:
            arrived = passed_along(outgoing, "section", 1)
    kept_stack = jax.tree.map(lambda *entries: jnp.stack(entries), *kept_rows)

    def run_input(incoming, kept_values, segment_row):
        return layer_backward(incoming, kept_values, gathered, segment_row)

    shard_total = tuple(
        (
            jnp.zeros(piece.shape[1:], jnp.float32)
            for piece in (
                norm1_gain,
                qkv_weight,
                qkv_bias,
                out_weight,
                norm2_gain,
                gate_weight,
                up_weight,
                down_weight,
            )
        )
    )
    small_total = (
        jnp.zeros((model_width,), jnp.float32),
        jnp.zeros((qkv_weight.shape[2],), jnp.float32),
        jnp.zeros((model_width,), jnp.float32),
    )
    pair_rows = []
    grad_rows = []
    arrived_grad = jnp.zeros((seq_length, model_width), jnp.bfloat16)
    for tick_step in range(micro_count + 1):
        micro_index = tick_step - 1 + section_index
        in_range = (micro_index >= 0) & (micro_index < micro_count)
        picked = jnp.clip(micro_index, 0, micro_count - 1)
        fresh_rows = out_grad[min(tick_step, micro_count - 1), 0]
        incoming = jnp.where(section_index == 1, fresh_rows, arrived_grad)
        forward_tick = jnp.clip(micro_index + section_index, 0, micro_count)
        kept_values = jax.tree.map(
            lambda stacked: lax.dynamic_index_in_dim(stacked, forward_tick, 0, keepdims=False),
            kept_stack,
        )
        segment_row = lax.dynamic_index_in_dim(segment_rows, picked, 0, keepdims=False)
        grad_stream, small_grads, operand_pairs = lax.cond(
            in_range, run_input, skipped(run_input), incoming, kept_values, segment_row
        )
        small_total = tuple((running + addend for running, addend in zip(small_total, small_grads)))
        pair_rows.append(operand_pairs)
        outgoing_grad = grad_stream.astype(jnp.bfloat16)
        grad_rows.append(outgoing_grad)
        if tick_step < micro_count:
            arrived_grad = passed_along(outgoing_grad, "section", -1)
    first_tick = 1 - section_index

    def valid_rows(stacked):
        chosen = lax.dynamic_slice_in_dim(stacked, first_tick, micro_count, 0)
        return chosen.reshape(-1, stacked.shape[-1])

    joined = jax.tree.map(lambda *entries: valid_rows(jnp.stack(entries)), *pair_rows)
    weight_grads = weight_pass(joined)
    shard_total = (
        lax.psum_scatter(small_total[0], "fsdp", scatter_dimension=0, tiled=True),
        lax.psum_scatter(weight_grads[0], "fsdp", scatter_dimension=0, tiled=True),
        lax.psum_scatter(small_total[1], "fsdp", scatter_dimension=0, tiled=True),
        lax.psum_scatter(weight_grads[1], "fsdp", scatter_dimension=0, tiled=True),
        lax.psum_scatter(small_total[2], "fsdp", scatter_dimension=0, tiled=True),
        lax.psum_scatter(weight_grads[2], "fsdp", scatter_dimension=0, tiled=True),
        lax.psum_scatter(weight_grads[3], "fsdp", scatter_dimension=0, tiled=True),
        lax.psum_scatter(weight_grads[4], "fsdp", scatter_dimension=0, tiled=True),
    )
    section_out = lax.dynamic_slice_in_dim(jnp.stack(section_rows), section_index, micro_count, 0)
    section_in_grad = lax.dynamic_slice_in_dim(
        jnp.stack(grad_rows), 1 - section_index, micro_count, 0
    )
    return (
        section_out.reshape(1, micro_count, 1, seq_length, model_width),
        section_in_grad.reshape(1, micro_count, 1, seq_length, model_width),
        shard_total[0][None],
        shard_total[1][None],
        shard_total[2][None],
        shard_total[3][None],
        shard_total[4][None],
        shard_total[5][None],
        shard_total[6][None],
        shard_total[7][None],
    )


def solution(mesh):
    in_specs = (
        P(None, "fsdp", None, None),
        P(None, "fsdp", None, None),
        P(None, "fsdp", None),
        P("section", "fsdp"),
        P("section", "fsdp", None),
        P("section", "fsdp"),
        P("section", "fsdp", None),
        P("section", "fsdp"),
        P("section", "fsdp", None),
        P("section", "fsdp", None),
        P("section", "fsdp", None),
    )
    out_specs = (
        P("section", None, "fsdp", None, None),
        P("section", None, "fsdp", None, None),
        P("section", "fsdp"),
        P("section", "fsdp", None),
        P("section", "fsdp"),
        P("section", "fsdp", None),
        P("section", "fsdp"),
        P("section", "fsdp", None),
        P("section", "fsdp", None),
        P("section", "fsdp", None),
    )
    return jax.shard_map(shards, mesh=mesh, in_specs=in_specs, out_specs=out_specs, check_vma=False)
```

profile of v0, /device:TPU:1, one launch (start us, length us, event | category | flops | bytes accessed | tf_op | source)
XLA Modules:
  0.0 1906.0 jit_solution(15602182714727169707)
XLA Ops:
  18.7 142.9 %all-reduce.17 = (bf16[896]{0:T(1024)(128)(2,1)S(1)}, bf16[1152]{0:T(1024)(128)(2,1)S(1)}, bf16[896]{0:T(1024)(128)(2,1)S(1)}) all-reduce(bf16[896]{0:T(1024)(128)(2,1)S(1)} %dynamic-update-slice, bf16[1152]{0:T(1024)(128)(2,1)S(1)} %dynamic-update-slice.1, ...), channel_id=2, replica_groups=mesh['section'=2,'fsdp'=64] {'fsdp'}, use_global_device_ids=true, to_apply=%add | all-reduce | flops 2944 | bytes 11776 | tf_op jit(solution)/shard_map/all_gather | solution.py:259
  163.9 62.5 %all-gather.14.cloned.1.call-done = bf16[1,896,1152]{2,0,1:T(2,128)(2,1)} async-done(((bf16[1,14,1152]{2,0,1:T(2,128)(2,1)}), bf16[1,896,1152]{2,0,1:T(2,128)(2,1)}) %all-gather.14.cloned.1.call-update) | async-done | bytes 2064400 | tf_op jit(solution)/shard_map/all_gather | solution.py:260
  230.1 121.5 %all-gather.18.cloned.1.call-done = bf16[1,896,4864]{2,0,1:T(2,128)(2,1)} async-done(((bf16[1,14,4864]{2,0,1:T(2,128)(2,1)}), bf16[1,896,4864]{2,0,1:T(2,128)(2,1)}) %all-gather.18.cloned.1.call-update) | async-done | bytes 8716304 | tf_op jit(solution)/shard_map/all_gather | solution.py:264
  351.6 11.6 copy.402
  363.2 113.2 %all-gather.20.cloned.1.call-done = bf16[1,896,4864]{2,0,1:T(2,128)(2,1)} async-done(((bf16[1,14,4864]{2,0,1:T(2,128)(2,1)}), bf16[1,896,4864]{2,0,1:T(2,128)(2,1)}) %all-gather.20.cloned.1.call-update) | async-done | bytes 8716304 | tf_op jit(solution)/shard_map/all_gather | solution.py:265
  476.5 11.5 copy.401
  488.0 113.8 %all-gather.22.cloned.1.call-done = bf16[1,4864,896]{2,0,1:T(2,128)(2,1)} async-done(((bf16[1,76,896]{2,0,1:T(2,128)(2,1)}), bf16[1,4864,896]{2,0,1:T(2,128)(2,1)}) %all-gather.22.cloned.1.call-update) | async-done | bytes 8716304 | tf_op jit(solution)/shard_map/all_gather | solution.py:266
  601.8 12.2 copy.400
  614.0 29.2 %conditional.6 = (bf16[128,896]{1,0:T(8,128)(2,1)}, bf16[1,128,896]{2,1,0:T(8,128)(2,1)}, f32[1,128,896]{2,1,0:T(8,128)}, f32[1,128,1]{1,2,0:T(1,128)}, bf16[1,1...) conditional(s32[]{:T(128)} %convert_element_type.666, ...), branch_computations={%region_0.1_spmd, %region_1.7_spmd} | conditional | flops 3886495488 | bytes 168586784 | solution.py:282
  662.0 32.3 %conditional.7 = (bf16[128,896]{1,0:T(8,128)(2,1)}, bf16[1,128,896]{2,1,0:T(8,128)(2,1)}, f32[1,128,896]{2,1,0:T(8,128)S(1)}, f32[1,128,1]{1,2,0:T(1,128)}, bf16...) conditional(s32[]{:T(128)} %convert_element_type.669, ...), branch_computations={%region_7.8_spmd, %region_8.14_spmd} | conditional | flops 3885348608 | bytes 167894528 | solution.py:282
  718.6 10.7 conditional.8
  752.3 11.3 conditional.9
  763.6 7.9 collective-permute-start.2
  772.5 45.7 %collective-permute-done.2 = bf16[128,896]{1,0:T(8,128)(2,1)} collective-permute-done((bf16[128,896]{1,0:T(8,128)(2,1)}, bf16[128,896]{1,0:T(8,128)(2,1)}, u32[]{:S(2)}, u32[]{:S(2)}) %collective-permute-start.2) | collective-permute-done | bytes 229408 | tf_op jit(solution)/shard_map/ppermute | solution.py:20
  818.2 49.4 %conditional.10 = (f32[896]{0:T(1024)S(1)}, f32[1152]{0:T(1024)S(1)}, f32[896]{0:T(1024)S(1)}, bf16[128,896]{1,0:T(8,128)(2,1)}, bf16[1,128,896]{2,1,0:T(8,128)(...) conditional(s32[]{:T(128)} %convert_element_type.674, ...), branch_computations={%region_30.31_spmd, %region_31.39_spmd} | conditional | flops 3981305856 | bytes 144260912 | solution.py:330
  822.6 9.2 fusion.154
  877.0 47.5 %conditional.11 = (f32[896]{0:T(1024)S(1)}, f32[1152]{0:T(1024)S(1)}, f32[896]{0:T(1024)S(1)}, bf16[1,128,896]{2,1,0:T(8,128)(2,1)}, bf16[1,128,896]{2,1,0:T(8,1...) conditional(s32[]{:T(128)} %convert_element_type.675, ...), branch_computations={%region_39.40_spmd, %region_40.48_spmd} | conditional | flops 3981305856 | bytes 139181664 | solution.py:330
  881.6 9.6 fusion.206
  925.2 9.8 convolution_bitcast_fusion.11
  935.0 10.4 convolution_bitcast_fusion.10
  953.4 264.4 %fusion.298 = (f32[16,1152]{1,0:T(8,128)S(1)}, f32[16,896]{1,0:T(8,128)S(1)}, f32[16,4864]{1,0:T(8,128)S(1)}, f32[16,4864]{1,0:T(8,128)S(1)}) fusion(f32[896,1152]{1,0:T(8,128)} %convolution_bitcast_fusion.12, f32[896,896]{1,0:T(8,128)} %convolution_bitcast_fusion.13, f32[896,4864]{1,0:T(8,128)} %convolution_bitcast_fusion.11, ...), kind=kCustom, calls=%all-reduce-scatter.5 | all-reduce-scatter fusion | flops 12058625 | bytes 42959360
  1217.9 6.7 collective-permute-start.18
  1230.3 10.6 convolution_bitcast_fusion.9
  1240.9 183.0 %fusion.4 = f32[80,896]{1,0:T(8,128)S(1)} fusion(f32[4864,896]{1,0:T(8,128)} %convolution_bitcast_fusion.9), kind=kCustom, calls=%all-reduce-scatter.4 | all-reduce-scatter fusion | flops 4587521 | bytes 17719808
  1431.7 6.6 collective-permute-start.14
  1466.5 14.1 collective-permute-start.27
  1481.4 269.2 %all-reduce.16 = (f32[896]{0:T(1024)S(1)}, f32[1152]{0:T(1024)S(1)}, f32[896]{0:T(1024)S(1)}) all-reduce(f32[896]{0:T(1024)S(1)} %add_add_fusion.2, f32[1152]{0:T(1024)S(1)} %add_add_fusion, f32[896]{0:T(1024)S(1)} %add_add_fusion.1), channel_id=10, replica_groups=mesh['section'=2,'fsdp'=64] {'fsdp'}, use_global_device_ids=true, to_apply=%region_48.49.clone | all-reduce | flops 2944 | bytes 23552
  1753.2 11.0 collective-permute-start.4
  1776.3 7.2 concatenate.397
  1800.0 7.8 collective-permute-start.35
  1821.7 26.6 %concatenate.398 = f32[142,4864]{1,0:T(8,128)} concatenate(f32[14,4864]{1,0:T(8,128)S(1)} %collective-permute-done.27, f32[16,4864]{1,0:T(8,128)S(1)} %copy-done.71, f32[16,4864]{1,0:T(8,128)S(1)} %copy-done.73, f32[16,4864]{1,0:T(8,128)} %copy-done.74, f32[16,4864]{1,0:T(8,128)} %collective-permute-done.23, f32[16,4864]{1,0:T(8,128)} %collective-permute-done.22, ...), dimensions={0} | concatenate | bytes 5525504
  1869.8 27.2 %concatenate.399 = f32[142,4864]{1,0:T(8,128)} concatenate(f32[14,4864]{1,0:T(8,128)} %collective-permute-done.35, f32[16,4864]{1,0:T(8,128)} %collective-permute-done.34, f32[16,4864]{1,0:T(8,128)} %collective-permute-done.33, f32[16,4864]{1,0:T(8,128)S(1)} %collective-permute-done.32, f32[16,4864]{1,0:T(8,128)S(1)} %collective-permute-done.31, ...), dimensions={0} | concatenate | bytes 5525504
  (645 shorter events, 367.9 us)
Async XLA Ops:
  7.2 154.5 %all-gather.16.cloned.1.call-start = ((), (), s32[]{:S(2)}) async-start(), calls=%async_computation.1 | async-start | bytes 3261440 | tf_op jit(solution)/shard_map/all_gather | solution.py:262
  8.7 217.6 %all-gather.14.cloned.1.call-start = ((), (), s32[]{:S(2)}) async-start(), calls=%async_computation | async-start | bytes 4193280 | tf_op jit(solution)/shard_map/all_gather | solution.py:260
  10.2 341.4 %all-gather.18.cloned.1.call-start = ((), (), s32[]{:S(2)}) async-start(), calls=%async_computation.2 | async-start | bytes 17704960 | tf_op jit(solution)/shard_map/all_gather | solution.py:264
  12.1 464.3 %all-gather.20.cloned.1.call-start = ((), (), s32[]{:S(2)}) async-start(), calls=%async_computation.3 | async-start | bytes 17704960 | tf_op jit(solution)/shard_map/all_gather | solution.py:265
  14.0 587.8 %all-gather.22.cloned.1.call-start = ((), (), s32[]{:S(2)}) async-start(), calls=%async_computation.4 | async-start | bytes 17704960 | tf_op jit(solution)/shard_map/all_gather | solution.py:266
  643.3 18.7 collective-permute-start
  694.3 24.2 %collective-permute-start.1 = (bf16[128,896]{1,0:T(8,128)(2,1)}, bf16[128,896]{1,0:T(8,128)(2,1)S(1)}, u32[]{:S(2)}, u32[]{:S(2)}) collective-permute-start(bf16[128,896]{1,0:T(8,128)(2,1)} %get-tuple-element.1394), channel_id=1, source_target_pairs={{0,64},{1,65},{2,66},{3,67},{4,68},{5,69},{6,70},{7,71},{8,72},{9,... | collective-permute-start | bytes 688136 | tf_op jit(solution)/shard_map/ppermute | solution.py:20
  763.6 54.6 %collective-permute-start.2 = (bf16[128,896]{1,0:T(8,128)(2,1)}, bf16[128,896]{1,0:T(8,128)(2,1)}, u32[]{:S(2)}, u32[]{:S(2)}) collective-permute-start(bf16[128,896]{1,0:T(8,128)(2,1)} %get-tuple-element.1439), channel_id=1, source_target_pairs={{64,0},{65,1},{66,2},{67,3},{68,4},{69,5},{70,6},{71,7},{72,8},{73... | collective-permute-start | bytes 688136 | tf_op jit(solution)/shard_map/ppermute | solution.py:20
  1217.9 220.4 %collective-permute-start.18 = (f32[16,896]{1,0:T(8,128)S(1)}, f32[16,896]{1,0:T(8,128)S(1)}, u32[]{:S(2)}, u32[]{:S(2)}) collective-permute-start(f32[16,896]{1,0:T(8,128)S(1)} %get-tuple-element.1774), channel_id=1, source_target_pairs={{0,7},{1,8},{2,9},{3,10},{4,11},{5,12},{6,13},{7,14},{8,15},{9,16}... | collective-permute-start | bytes 172040
  1224.6 215.0 %collective-permute-start.17 = (f32[16,896]{1,0:T(8,128)S(1)}, f32[16,896]{1,0:T(8,128)S(1)}, u32[]{:S(2)}, u32[]{:S(2)}) collective-permute-start(f32[16,896]{1,0:T(8,128)S(1)} %get-tuple-element.1774), channel_id=1, source_target_pairs={{0,6},{1,7},{2,8},{3,9},{4,10},{5,11},{6,12},{7,13},{8,14},{9,15},... | collective-permute-start | bytes 172040
  1225.9 205.8 %collective-permute-start.19 = (f32[14,896]{1,0:T(8,128)S(1)}, f32[14,896]{1,0:T(8,128)S(1)}, u32[]{:S(2)}, u32[]{:S(2)}) collective-permute-start(f32[14,896]{1,0:T(8,128)S(1)} %slice.289), channel_id=1, source_target_pairs={{0,8},{1,9},{2,10},{3,11},{4,12},{5,13},{6,14},{7,15},{8,16},{9,17... | collective-permute-start | bytes 150536
  1427.7 15.2 collective-permute-start.16
  1429.0 15.2 collective-permute-start.15
  1445.5 17.5 collective-permute-start.8
  1446.9 19.6 %collective-permute-start.7 = (f32[16,1152]{1,0:T(8,128)S(1)}, f32[16,1152]{1,0:T(8,128)S(1)}, u32[]{:S(2)}, u32[]{:S(2)}) collective-permute-start(f32[16,1152]{1,0:T(8,128)S(1)} %get-tuple-element.1773), channel_id=1, source_target_pairs={{0,4},{1,5},{2,6},{3,7},{4,8},{5,9},{6,10},{7,11},{8,12},{9,13},{1... | collective-permute-start | bytes 221192
  1451.5 299.0 %collective-permute-start.6 = (f32[16,1152]{1,0:T(8,128)S(1)}, f32[16,1152]{1,0:T(8,128)S(1)}, u32[]{:S(2)}, u32[]{:S(2)}) collective-permute-start(f32[16,1152]{1,0:T(8,128)S(1)} %get-tuple-element.1773), channel_id=1, source_target_pairs={{0,3},{1,4},{2,5},{3,6},{4,7},{5,8},{6,9},{7,10},{8,11},{9,12},{10... | collective-permute-start | bytes 221192
  1455.3 312.9 %collective-permute-start.38 = (f32[80,896]{1,0:T(8,128)S(1)}, f32[80,896]{1,0:T(8,128)}, u32[]{:S(2)}, u32[]{:S(2)}) collective-permute-start(f32[80,896]{1,0:T(8,128)S(1)} %fusion.4), channel_id=1, source_target_pairs={{0,3},{1,4},{2,5},{3,6},{4,7},{5,8},{6,9},{7,10},{8,11},{9,12},{10... | collective-permute-start | bytes 860168
  1458.9 310.7 %collective-permute-start.37 = (f32[80,896]{1,0:T(8,128)S(1)}, f32[80,896]{1,0:T(8,128)}, u32[]{:S(2)}, u32[]{:S(2)}) collective-permute-start(f32[80,896]{1,0:T(8,128)S(1)} %fusion.4), channel_id=1, source_target_pairs={{0,2},{1,3},{2,4},{3,5},{4,6},{5,7},{6,8},{7,9},{8,10},{9,11},{10,... | collective-permute-start | bytes 860168
  1463.0 308.6 %collective-permute-start.36 = (f32[80,896]{1,0:T(8,128)S(1)}, f32[80,896]{1,0:T(8,128)}, u32[]{:S(2)}, u32[]{:S(2)}) collective-permute-start(f32[80,896]{1,0:T(8,128)S(1)} %fusion.4), channel_id=1, source_target_pairs={{0,1},{1,2},{2,3},{3,4},{4,5},{5,6},{6,7},{7,8},{8,9},{9,10},{10,1... | collective-permute-start | bytes 860168
  1466.5 300.4 %collective-permute-start.27 = (f32[14,4864]{1,0:T(8,128)S(1)}, f32[14,4864]{1,0:T(8,128)S(1)}, u32[]{:S(2)}, u32[]{:S(2)}) collective-permute-start(f32[14,4864]{1,0:T(8,128)S(1)} %slice.290), channel_id=1, source_target_pairs={{0,8},{1,9},{2,10},{3,11},{4,12},{5,13},{6,14},{7,15},{8,16},{9,17... | collective-permute-start | bytes 817160
  1765.6 24.0 %collective-permute-start.26 = (f32[16,4864]{1,0:T(8,128)S(1)}, f32[16,4864]{1,0:T(8,128)S(1)}, u32[]{:S(2)}, u32[]{:S(2)}) collective-permute-start(f32[16,4864]{1,0:T(8,128)S(1)} %get-tuple-element.1775), channel_id=1, source_target_pairs={{0,7},{1,8},{2,9},{3,10},{4,11},{5,12},{6,13},{7,14},{8,15},{9,16}... | collective-permute-start | bytes 933896
  1766.9 24.8 %collective-permute-start.25 = (f32[16,4864]{1,0:T(8,128)S(1)}, f32[16,4864]{1,0:T(8,128)S(1)}, u32[]{:S(2)}, u32[]{:S(2)}) collective-permute-start(f32[16,4864]{1,0:T(8,128)S(1)} %get-tuple-element.1775), channel_id=1, source_target_pairs={{0,6},{1,7},{2,8},{3,9},{4,10},{5,11},{6,12},{7,13},{8,14},{9,15},... | collective-permute-start | bytes 933896
  1768.2 27.7 %collective-permute-start.24 = (f32[16,4864]{1,0:T(8,128)S(1)}, f32[16,4864]{1,0:T(8,128)S(1)}, u32[]{:S(2)}, u32[]{:S(2)}) collective-permute-start(f32[16,4864]{1,0:T(8,128)S(1)} %get-tuple-element.1775), channel_id=1, source_target_pairs={{0,5},{1,6},{2,7},{3,8},{4,9},{5,10},{6,11},{7,12},{8,13},{9,14},{... | collective-permute-start | bytes 933896
  1769.6 28.4 %collective-permute-start.23 = (f32[16,4864]{1,0:T(8,128)S(1)}, f32[16,4864]{1,0:T(8,128)}, u32[]{:S(2)}, u32[]{:S(2)}) collective-permute-start(f32[16,4864]{1,0:T(8,128)S(1)} %get-tuple-element.1775), channel_id=1, source_target_pairs={{0,4},{1,5},{2,6},{3,7},{4,8},{5,9},{6,10},{7,11},{8,12},{9,13},{1... | collective-permute-start | bytes 933896
  1771.6 28.4 %collective-permute-start.22 = (f32[16,4864]{1,0:T(8,128)S(1)}, f32[16,4864]{1,0:T(8,128)}, u32[]{:S(2)}, u32[]{:S(2)}) collective-permute-start(f32[16,4864]{1,0:T(8,128)S(1)} %get-tuple-element.1775), channel_id=1, source_target_pairs={{0,3},{1,4},{2,5},{3,6},{4,7},{5,8},{6,9},{7,10},{8,11},{9,12},{10... | collective-permute-start | bytes 933896
  1789.6 24.3 %collective-permute-start.21 = (f32[16,4864]{1,0:T(8,128)S(1)}, f32[16,4864]{1,0:T(8,128)}, u32[]{:S(2)}, u32[]{:S(2)}) collective-permute-start(f32[16,4864]{1,0:T(8,128)S(1)} %get-tuple-element.1775), channel_id=1, source_target_pairs={{0,2},{1,3},{2,4},{3,5},{4,6},{5,7},{6,8},{7,9},{8,10},{9,11},{10,... | collective-permute-start | bytes 933896
  1791.7 23.5 %collective-permute-start.20 = (f32[16,4864]{1,0:T(8,128)S(1)}, f32[16,4864]{1,0:T(8,128)}, u32[]{:S(2)}, u32[]{:S(2)}) collective-permute-start(f32[16,4864]{1,0:T(8,128)S(1)} %get-tuple-element.1775), channel_id=1, source_target_pairs={{0,1},{1,2},{2,3},{3,4},{4,5},{5,6},{6,7},{7,8},{8,9},{9,10},{10,1... | collective-permute-start | bytes 933896
  1795.9 58.8 %collective-permute-start.34 = (f32[16,4864]{1,0:T(8,128)S(1)}, f32[16,4864]{1,0:T(8,128)}, u32[]{:S(2)}, u32[]{:S(2)}) collective-permute-start(f32[16,4864]{1,0:T(8,128)S(1)} %get-tuple-element.1776), channel_id=1, source_target_pairs={{0,7},{1,8},{2,9},{3,10},{4,11},{5,12},{6,13},{7,14},{8,15},{9,16}... | collective-permute-start | bytes 933896
  1798.0 58.5 %collective-permute-start.33 = (f32[16,4864]{1,0:T(8,128)S(1)}, f32[16,4864]{1,0:T(8,128)}, u32[]{:S(2)}, u32[]{:S(2)}) collective-permute-start(f32[16,4864]{1,0:T(8,128)S(1)} %get-tuple-element.1776), channel_id=1, source_target_pairs={{0,6},{1,7},{2,8},{3,9},{4,10},{5,11},{6,12},{7,13},{8,14},{9,15},... | collective-permute-start | bytes 933896
  1800.0 48.3 %collective-permute-start.35 = (f32[14,4864]{1,0:T(8,128)S(1)}, f32[14,4864]{1,0:T(8,128)}, u32[]{:S(2)}, u32[]{:S(2)}) collective-permute-start(f32[14,4864]{1,0:T(8,128)S(1)} %slice.291), channel_id=1, source_target_pairs={{0,8},{1,9},{2,10},{3,11},{4,12},{5,13},{6,14},{7,15},{8,16},{9,17... | collective-permute-start | bytes 817160
  1813.9 48.7 %collective-permute-start.32 = (f32[16,4864]{1,0:T(8,128)S(1)}, f32[16,4864]{1,0:T(8,128)S(1)}, u32[]{:S(2)}, u32[]{:S(2)}) collective-permute-start(f32[16,4864]{1,0:T(8,128)S(1)} %get-tuple-element.1776), channel_id=1, source_target_pairs={{0,5},{1,6},{2,7},{3,8},{4,9},{5,10},{6,11},{7,12},{8,13},{9,14},{... | collective-permute-start | bytes 933896
  1815.2 47.4 %collective-permute-start.31 = (f32[16,4864]{1,0:T(8,128)S(1)}, f32[16,4864]{1,0:T(8,128)S(1)}, u32[]{:S(2)}, u32[]{:S(2)}) collective-permute-start(f32[16,4864]{1,0:T(8,128)S(1)} %get-tuple-element.1776), channel_id=1, source_target_pairs={{0,4},{1,5},{2,6},{3,7},{4,8},{5,9},{6,10},{7,11},{8,12},{9,13},{1... | collective-permute-start | bytes 933896
  (144 other events, 4796.5 us)
Sparse Core Ops, SparseCore 0:
  10.3 108.6 all-gather.15
  121.4 104.9 all-gather.13
  228.6 122.9 all-gather.17
  353.8 122.6 all-gather.19
  478.6 123.1 all-gather.21
where the time goes:
time: 1920 us; the launch traced here: 1910 us
  blocking collectives  859 us (45%)
  waiting for transfers between devices  472 us (25%)
  local copies, waits for them, and re-layouts  253 us (13%)
  starting transfers between devices  135 us (7%)
  matrix products  126 us (7%)
  other arithmetic  39.4 us (2%)
  between operations  19.3 us (1%)
    unnamed x3, blocking collectives  717 us
    unnamed x159, local copies, waits for them, and re-layouts  167 us
    all_gather x1, blocking collectives, shards(): lax.all_gather(norm1_gain[0], 'fsdp', axis=0, tiled=True)  143 us
    unnamed x36, starting transfers between devices  123 us
    all_gather x1, waiting for transfers between devices, shards(): lax.all_gather(gate_weight[0], 'fsdp', axis=0, tiled=True)  122 us
    all_gather x1, waiting for transfers between devices, shards(): lax.all_gather(down_weight[0], 'fsdp', axis=0, tiled=True)  114 us
    all_gather x1, waiting for transfers between devices, shards(): lax.all_gather(up_weight[0], 'fsdp', axis=0, tiled=True)  113 us
    all_gather x1, waiting for transfers between devices, shards(): lax.all_gather(qkv_weight[0], 'fsdp', axis=0, tiled=True)  62.5 us
  transfers between devices with their start and end apart: 45, of which 11 were waited for; matrix products, arithmetic and copies ran while one was open for 17% of the time, Pallas kernels for 0%

commit v1 on v0

v1 whole, which is shorter than its diff:
```python
import math

import jax
import jax.numpy as jnp
from jax import lax
from jax.experimental import pallas as pl
from jax.experimental.pallas import tpu as pltpu
from jax.sharding import PartitionSpec as P

HEADS = 14
KV_HEADS = 2
HEAD_DIM = 64
MICRO = 2
SEQ = 128
D = 896
DP = 1024
QKV = 1152
norm_epsilon = 1e-06
rope_base = 1000000.0

MESH = pl.DeviceIdType.MESH
BF = jnp.bfloat16
F32 = jnp.float32


class Place:
    def __init__(self):
        f = lax.axis_index("fsdp")
        self.s = lax.axis_index("section")
        self.c = lax.rem(f, 2)
        self.z = lax.rem(f // 2, 4)
        self.y = lax.rem(f // 8, 2)
        self.x = f // 16

    def at(self, x=None, y=None, z=None, c=None):
        x = self.x if x is None else x
        y = self.y if y is None else y
        z = self.z if z is None else z
        c = self.c if c is None else c
        return (self.s, ((x * 2 + y) * 4 + z) * 2 + c)

    def step(self, axis, k):
        here = self.x if axis == "x" else self.z
        return lax.rem(here + (k + 4), 4)

    def to(self, axis, k):
        return self.at(**{axis: self.step(axis, k)})

    def across(self):
        return self.at(y=1 - self.y)

    def mate(self):
        return self.at(c=1 - self.c)


def greet(place):
    barrier = pltpu.get_barrier_semaphore()
    near = (
        place.to("x", 1), place.to("x", -1), place.to("z", 1), place.to("z", -1),
        place.across(), place.mate(),
    )
    for device in near:
        pl.semaphore_signal(barrier, inc=1, device_id=device, device_id_type=MESH)
    pl.semaphore_wait(barrier, len(near))


class Wire:
    def __init__(self, send_sems, recv_sems):
        self.send_sems, self.recv_sems, self.started = send_sems, recv_sems, []

    def send(self, src, dst, device):
        k = len(self.started)
        assert k < self.send_sems.shape[0]
        copy = pltpu.make_async_remote_copy(
            src_ref=src, dst_ref=dst, send_sem=self.send_sems.at[k],
            recv_sem=self.recv_sems.at[k], device_id=device, device_id_type=MESH,
        )
        copy.start()
        self.started.append(copy)
        return copy

    def drain(self):
        for copy in self.started:
            copy.wait_send()


def interleave(flows):
    waiting = [(next(flow), k, flow) for k, flow in enumerate(flows)]
    while waiting:
        waiting.sort(key=lambda item: item[:2])
        _, k, flow = waiting.pop(0)
        try:
            waiting.append((next(flow), k, flow))
        except StopIteration:
            pass


def gather_yab(wire, place, slot, first, last, ready, t0, unit):
    x, y, z = place.x, place.y, place.z
    yield t0
    for wait in ready:
        wait()
    cross = wire.send(slot(x, y, z), slot(x, y, z), place.across())

    def pos(a, b):
        return (b, a) if first == "z" else (a, b)

    def piece(a, b, half=None):
        px, pz = pos(a, b)
        return slot(px, half, pz)

    mine = {"x": x, "z": z}
    a0, b0 = mine[first], mine[last]
    t = t0 + unit * 1
    yield t
    cross.wait_recv()
    a_r = wire.send(piece(a0, b0), piece(a0, b0), place.to(first, 1))
    a_l = wire.send(piece(a0, b0), piece(a0, b0), place.to(first, -1))

    def last_sends(a):
        r = wire.send(piece(a, b0), piece(a, b0), place.to(last, 1))
        l = wire.send(piece(a, b0), piece(a, b0), place.to(last, -1))
        return r, l

    def last_forward(a, r, l):
        r.wait_recv()
        bm = place.step(last, -1)
        r2 = wire.send(piece(a, bm, 0), piece(a, bm, 0), place.to(last, 1))
        l.wait_recv()
        bp = place.step(last, 1)
        l2 = wire.send(piece(a, bp, 1), piece(a, bp, 1), place.to(last, -1))
        return r2, l2

    w0 = last_sends(a0)
    t += unit * 2
    yield t
    a_r.wait_recv()
    am = place.step(first, -1)
    a_r2 = wire.send(piece(am, b0, 0), piece(am, b0, 0), place.to(first, 1))
    a_l.wait_recv()
    ap = place.step(first, 1)
    a_l2 = wire.send(piece(ap, b0, 1), piece(ap, b0, 1), place.to(first, -1))
    w1 = last_sends(am)
    w2 = last_sends(ap)
    t += unit * 2
    yield t
    f0 = last_forward(a0, *w0)
    t += unit * 2
    yield t
    a_r2.wait_recv()
    a_l2.wait_recv()
    aq = place.step(first, 2)
    w3 = last_sends(aq)
    t += unit * 2
    yield t
    f1 = last_forward(am, *w1)
    t += unit * 2
    yield t
    f2 = last_forward(ap, *w2)
    t += unit * 2
    yield t
    f3 = last_forward(aq, *w3)
    t += unit * 2
    yield t
    for pair in (f0, f1, f2, f3):
        for copy in pair:
            copy.wait_recv()


def gather_aby(wire, place, slot, parts, t0, unit):
    x, y, z = place.x, place.y, place.z
    yield t0
    r = wire.send(slot(x, y, z), slot(x, y, z), place.to("x", 1))
    l = wire.send(slot(x, y, z), slot(x, y, z), place.to("x", -1))
    t = t0 + unit
    yield t
    r.wait_recv()
    xm, xp = place.step("x", -1), place.step("x", 1)
    r2 = wire.send(parts(xm, y, z, 0), parts(xm, y, z, 0), place.to("x", 1))
    l.wait_recv()
    l2 = wire.send(parts(xp, y, z, 1), parts(xp, y, z, 1), place.to("x", -1))
    t += unit
    yield t
    r2.wait_recv()
    l2.wait_recv()
    zr = wire.send(slot(None, y, z), slot(None, y, z), place.to("z", 1))
    zl = wire.send(slot(None, y, z), slot(None, y, z), place.to("z", -1))
    y0 = wire.send(slot(None, y, z), slot(None, y, z), place.across())
    t += unit * 4
    yield t
    zm, zp, zq = place.step("z", -1), place.step("z", 1), place.step("z", 2)
    zr.wait_recv()
    zr2 = wire.send(slot(0, y, zm), slot(0, y, zm), place.to("z", 1))
    y1 = wire.send(slot(None, y, zm), slot(None, y, zm), place.across())
    zl.wait_recv()
    zl2 = wire.send(slot(1, y, zp), slot(1, y, zp), place.to("z", -1))
    y2 = wire.send(slot(None, y, zp), slot(None, y, zp), place.across())
    t += unit * 4
    yield t
    zr2.wait_recv()
    zl2.wait_recv()
    y3 = wire.send(slot(None, y, zq), slot(None, y, zq), place.across())
    t += unit * 10
    yield t
    for copy in (y0, y1, y2, y3):
        copy.wait_recv()


N_AG = 104
AG_COLS = dict(G=2560, U=2560, D=896, Q=1152, O=896)
BLOCK = dict(G=(32, 2560), U=(32, 2560), D=(80, 896), Q=(32, 1152), O=(32, 896))


def gather_flows(wire, place, ins, bufs, local_sems):
    x, y, z, c = place.x, place.y, place.z, place.c
    rows = pl.ds(pl.multiple_of(c * 16, 16), 16)
    G, U, D, Q, O = bufs
    g_in, u_in, d_in, q_in, o_in = ins
    own = []
    for k, (src, dst) in enumerate((
        (g_in.at[c], G.at[x, y, z, rows]), (u_in.at[c], U.at[x, y, z, rows]),
        (d_in, D.at[x, y, z]), (q_in, Q.at[x, y, z, rows]), (o_in, O.at[x, y, z, rows]),
    )):
        copy = pltpu.make_async_copy(src, dst, local_sems.at[k])
        copy.start()
        own.append(copy)
    swap_g = wire.send(g_in.at[1 - c], G.at[x, y, z, rows], place.mate())
    swap_u = wire.send(u_in.at[1 - c], U.at[x, y, z, rows], place.mate())

    def whole(buf):
        def slot(px, half, pz):
            if half is None:
                return buf.at[px, :, pz]
            return buf.at[px, half, pz]
        return slot

    def part(buf):
        def slot(px, half, pz):
            if half is None:
                return buf.at[px, :, pz, rows]
            return buf.at[px, half, pz, rows]
        return slot

    def down_slot(px, py, pz):
        if px is None:
            return D.at[:, py, pz]
        return D.at[px, py, pz]

    def down_zslot(px, py, pz):
        if px is None:
            return D.at[:, py, pz]
        if isinstance(px, int):
            return D.at[pl.ds(2 * px, 2), py, pz]
        return D.at[px, py, pz]

    def down_parts(px, py, pz, half):
        r = pl.ds(0, 48) if half == 0 else pl.ds(48, 32)
        return D.at[px, py, pz, r]

    def attention(buf, k, t0):
        yield from gather_yab(wire, place, part(buf), "z", "x", (own[k].wait,), t0, 1.0)
        mine = buf.at[:, :, :, rows]
        swap = wire.send(mine, mine, place.mate())
        yield 100.0
        swap.wait_recv()

    def down(t0):
        yield t0
        own[2].wait()
        yield from gather_aby(wire, place, down_zslot, down_parts, t0, 2.0)

    flows = [
        attention(Q, 3, 0.0),
        attention(O, 4, 0.1),
        down(0.2),
        gather_yab(wire, place, whole(G), "z", "x", (own[0].wait, swap_g.wait_recv), 0.3, 4.0),
        gather_yab(wire, place, whole(U), "x", "z", (own[1].wait, swap_u.wait_recv), 0.4, 4.0),
    ]
    return flows


def ag_kernel(g_in, u_in, d_in, q_in, o_in, g_o, u_o, d_o, q_o, o_o, G, U, D, Q, O, ss, rs, ls):
    place = Place()
    greet(place)
    wire = Wire(ss, rs)
    interleave(gather_flows(wire, place, (g_in, u_in, d_in, q_in, o_in), (G, U, D, Q, O), ls))
    wire.drain()
    out = []
    for k, (src, dst) in enumerate(((G, g_o), (U, u_o), (D, d_o), (Q, q_o), (O, o_o))):
        copy = pltpu.make_async_copy(src, dst, ls.at[k])
        copy.start()
        out.append(copy)
    for copy in out:
        copy.wait()


def bufs_shapes():
    return [(4, 2, 4) + BLOCK[k] for k in "GUDQO"]


def all_gather_weights(g, u, d, q, o):
    shapes = bufs_shapes()
    return pl.pallas_call(
        ag_kernel,
        out_shape=[jax.ShapeDtypeStruct(s, BF) for s in shapes],
        in_specs=[pl.BlockSpec(memory_space=pltpu.VMEM)] * 5,
        out_specs=[pl.BlockSpec(memory_space=pl.ANY)] * 5,
        scratch_shapes=[pltpu.VMEM(s, BF) for s in shapes]
        + [pltpu.SemaphoreType.DMA((N_AG,)), pltpu.SemaphoreType.DMA((N_AG,)), pltpu.SemaphoreType.DMA((5,))],
        compiler_params=pltpu.CompilerParams(
            collective_id=0, has_side_effects=True, vmem_limit_bytes=60 * 2**20
        ),
        name="gather_weights",
    )(g, u, d, q, o)


def add(dst, *srcs):
    total = dst[...]
    for src in srcs:
        total = total + src[...]
    dst[...] = total


def add_each(count, dst, *srcs):
    def body(i, carry):
        add(dst(i), *[src(i) for src in srcs])
        return carry
    lax.fori_loop(0, count, body, 0)


def scatter_aby(wire, place, slot, R, first, last, ready, t0, unit):
    r1a, r1b, r2a, r2b, s1a, s1b, s2a, s2b, t_buf = R
    mine = {"x": place.x, "z": place.z}
    a0, b0 = mine[first], mine[last]

    def piece(a, b, half=None):
        return slot(b, half, a) if first == "z" else slot(a, half, b)

    def blocks(a, b):
        return lambda i: piece(a, b, i)

    ap, am, aq = place.step(first, 1), place.step(first, -1), place.step(first, 2)
    order = [place.step(last, k) for k in (2, 1, -1)] + [b0]
    t = t0
    yield t
    for wait in ready:
        wait()
    one = []
    for k, b in enumerate(order):
        one.append((
            wire.send(piece(aq, b, 0), r1a.at[k], place.to(first, 1)),
            wire.send(piece(aq, b, 1), r1b.at[k], place.to(first, -1)),
        ))
    two = []
    for k, b in enumerate(order):
        t = t0 + unit * (k + 1)
        yield t
        one[k][0].wait_recv()
        add(piece(ap, b, 0), r1a.at[k])
        right = wire.send(piece(ap, b), r2a.at[k], place.to(first, 1))
        one[k][1].wait_recv()
        add(piece(am, b, 1), r1b.at[k])
        left = wire.send(piece(am, b), r2b.at[k], place.to(first, -1))
        two.append((right, left))
    t1 = t0 + unit * 4
    bp, bm, bq = order[1], order[2], order[0]

    def settle(k):
        two[k][0].wait_recv()
        two[k][1].wait_recv()
        for i in range(2):
            add(piece(a0, order[k], i), r2a.at[k, i], r2b.at[k, i])

    yield t1 + 2 * unit
    settle(0)
    d_r = wire.send(piece(a0, bq, 0), s1a, place.to(last, 1))
    d_l = wire.send(piece(a0, bq, 1), s1b, place.to(last, -1))
    yield t1 + 4 * unit
    settle(1)
    d_r.wait_recv()
    add(piece(a0, bp, 0), s1a)
    e_r = wire.send(piece(a0, bp), s2a, place.to(last, 1))
    yield t1 + 6 * unit
    settle(2)
    d_l.wait_recv()
    add(piece(a0, bm, 1), s1b)
    e_l = wire.send(piece(a0, bm), s2b, place.to(last, -1))
    yield t1 + 8 * unit
    settle(3)
    yield t1 + 9 * unit
    e_r.wait_recv()
    e_l.wait_recv()
    for i in range(2):
        add(piece(a0, b0, i), s2a.at[i], s2b.at[i])
    other = slot(place.x, 1 - place.y, place.z)
    cross = wire.send(other, t_buf, place.across())
    yield t1 + 10 * unit
    cross.wait_recv()
    add(slot(place.x, place.y, place.z), t_buf)


def scatter_down(wire, place, D, R, ready, t0, unit):
    yb, z1a, z1b, z2a, z2b, xa, xb, x2a, x2b = R
    x, y, z = place.x, place.y, place.z
    zp, zm, zq = place.step("z", 1), place.step("z", -1), place.step("z", 2)
    xp, xm, xq = place.step("x", 1), place.step("x", -1), place.step("x", 2)
    top, low = pl.ds(0, 48), pl.ds(48, 32)
    lo, hi = pl.ds(0, 2), pl.ds(2, 2)
    order = (zq, zp, zm, z)
    yield t0
    for wait in ready:
        wait()
    crossing = [wire.send(D.at[:, 1 - y, b], yb.at[k], place.across()) for k, b in enumerate(order)]

    def settle(k):
        crossing[k].wait_recv()
        add_each(4, lambda i: D.at[i, y, order[k]], lambda i: yb.at[k, i])

    yield t0 + 3 * unit
    settle(0)
    d_r = wire.send(D.at[lo, y, zq], z1a, place.to("z", 1))
    d_l = wire.send(D.at[hi, y, zq], z1b, place.to("z", -1))
    yield t0 + 6 * unit
    settle(1)
    d_r.wait_recv()
    add_each(2, lambda i: D.at[i, y, zp], lambda i: z1a.at[i])
    e_r = wire.send(D.at[:, y, zp], z2a, place.to("z", 1))
    yield t0 + 9 * unit
    settle(2)
    d_l.wait_recv()
    add_each(2, lambda i: D.at[i + 2, y, zm], lambda i: z1b.at[i])
    e_l = wire.send(D.at[:, y, zm], z2b, place.to("z", -1))
    yield t0 + 12 * unit
    settle(3)
    yield t0 + 13 * unit
    e_r.wait_recv()
    e_l.wait_recv()
    add_each(4, lambda i: D.at[i, y, z], lambda i: z2a.at[i], lambda i: z2b.at[i])
    f_r = wire.send(D.at[xq, y, z, top], xa, place.to("x", 1))
    f_l = wire.send(D.at[xq, y, z, low], xb, place.to("x", -1))
    yield t0 + 14 * unit
    f_r.wait_recv()
    add(D.at[xp, y, z, top], xa)
    g_r = wire.send(D.at[xp, y, z], x2a, place.to("x", 1))
    f_l.wait_recv()
    add(D.at[xm, y, z, low], xb)
    g_l = wire.send(D.at[xm, y, z], x2b, place.to("x", -1))
    yield t0 + 15 * unit
    g_r.wait_recv()
    g_l.wait_recv()
    add(D.at[x, y, z], x2a, x2b)


def rs_scratch():
    def aby(rows, cols):
        shapes = [(4, rows, cols)] * 2 + [(4, 2, rows, cols)] * 2 + [(rows, cols)] * 2 + [(2, rows, cols)] * 2 + [(rows, cols)]
        return [pltpu.VMEM(s, BF) for s in shapes]
    out = []
    out += aby(32, 2560) + [pltpu.VMEM((16, 2560), BF)]
    out += aby(32, 2560) + [pltpu.VMEM((16, 2560), BF)]
    b = (80, 896)
    out += [pltpu.VMEM(s, BF) for s in (
        (4, 4) + b, (2,) + b, (2,) + b, (4,) + b, (4,) + b, (48, 896), (32, 896), b, b)]
    out += aby(16, 1152) + [pltpu.VMEM((4, 2, 4, 16, 1152), BF)]
    out += aby(16, 896) + [pltpu.VMEM((4, 2, 4, 16, 896), BF)]
    return out


N_RS_SCRATCH = 10 + 10 + 9 + 10 + 10
N_RS = 104


def scatter_flows(wire, place, bufs, R, ready, outs, times):
    x, y, z, c = place.x, place.y, place.z, place.c
    G, U, D, Q, O = bufs
    g_o, u_o, d_o, q_o, o_o = outs
    rg, ru, rd, rq, ro = R[:10], R[10:20], R[20:29], R[29:39], R[39:49]
    rows = pl.ds(pl.multiple_of(c * 16, 16), 16)
    others = pl.ds(pl.multiple_of(16 - c * 16, 16), 16)

    def whole(buf):
        def slot(px, half, pz):
            return buf.at[px, :, pz] if half is None else buf.at[px, half, pz]
        return slot

    def part(buf):
        def slot(px, half, pz):
            return buf.at[px, :, pz, rows] if half is None else buf.at[px, half, pz, rows]
        return slot

    def hidden(buf, out, r, first, last, ready, t0):
        yield from scatter_aby(wire, place, whole(buf), r[:9], first, last, ready, t0, 4.0)
        swap = wire.send(buf.at[x, y, z, others], r[9], place.mate())
        yield 200.0
        swap.wait_recv()
        out[c] = buf[x, y, z, rows].astype(F32)
        out[1 - c] = r[9][...].astype(F32)

    def attention(buf, out, r, ready, t0):
        yield t0
        for wait in ready:
            wait()
        swap = wire.send(buf.at[:, :, :, others], r[9], place.mate())
        yield t0 + 8.0
        swap.wait_recv()
        add_each(32, lambda i: buf.at[i // 8, lax.rem(i // 4, 2), lax.rem(i, 4), rows],
                 lambda i: r[9].at[i // 8, lax.rem(i // 4, 2), lax.rem(i, 4)])
        yield from scatter_aby(wire, place, part(buf), r[:9], "x", "z", (), t0 + 8.0, 1.0)
        out[...] = buf[x, y, z, rows].astype(F32)

    def down(t0):
        yield from scatter_down(wire, place, D, rd, ready[2], t0, 4.0)
        d_o[...] = D[x, y, z].astype(F32)

    return [
        down(times[2]),
        hidden(G, g_o, rg, "x", "z", ready[0], times[0]),
        hidden(U, u_o, ru, "z", "x", ready[1], times[1]),
        attention(O, o_o, ro, ready[4], times[4]),
        attention(Q, q_o, rq, ready[3], times[3]),
    ]


def rs_kernel(*refs):
    ins, outs, bufs = refs[:5], refs[5:10], refs[10:15]
    R = refs[15:15 + N_RS_SCRATCH]
    ss, rs, ls = refs[15 + N_RS_SCRATCH:]
    place = Place()
    loads = []
    for k in (2, 0, 1, 4, 3):
        copy = pltpu.make_async_copy(ins[k], bufs[k], ls.at[k])
        copy.start()
        loads.append((k, copy))
    ready = {k: (copy.wait,) for k, copy in loads}
    greet(place)
    wire = Wire(ss, rs)
    interleave(scatter_flows(wire, place, bufs, R, ready, outs, (0.1, 0.2, 0.0, 0.4, 0.3)))
    wire.drain()


def reduce_scatter_grads(g, u, d, q, o):
    shapes = bufs_shapes()
    return pl.pallas_call(
        rs_kernel,
        out_shape=[jax.ShapeDtypeStruct(s, F32) for s in ((2, 16, 2560), (2, 16, 2560), (80, 896), (16, 1152), (16, 896))],
        in_specs=[pl.BlockSpec(memory_space=pl.ANY)] * 5,
        out_specs=[pl.BlockSpec(memory_space=pltpu.VMEM)] * 5,
        scratch_shapes=[pltpu.VMEM(s, BF) for s in shapes] + rs_scratch()
        + [pltpu.SemaphoreType.DMA((N_RS,)), pltpu.SemaphoreType.DMA((N_RS,)), pltpu.SemaphoreType.DMA((5,))],
        compiler_params=pltpu.CompilerParams(
            collective_id=1, has_side_effects=True, vmem_limit_bytes=60 * 2**20
        ),
        name="scatter_grads",
    )(g, u, d, q, o)


def rope_tables(segment_row, head_size):
    length = segment_row.shape[0]
    places = jnp.arange(length, dtype=jnp.int32)
    changes = jnp.concatenate(
        [jnp.ones((1,), jnp.int32), (segment_row[1:] != segment_row[:-1]).astype(jnp.int32)]
    )
    starts = lax.cummax(places * changes, axis=0)
    offsets = (places - starts).astype(F32)
    ladder = jnp.arange(head_size // 2, dtype=F32) * (-2.0 * math.log(rope_base) / head_size)
    angles = offsets[:, None] * jnp.exp(ladder)[None, :]
    angles = jnp.concatenate([angles, angles], axis=-1)
    return (jnp.cos(angles), jnp.sin(angles))


def rotate_half(head_block):
    half_width = head_block.shape[-1] // 2
    return jnp.concatenate([-head_block[..., half_width:], head_block[..., :half_width]], axis=-1)


def spin(head_block, cosine_table, sine_table):
    return head_block * cosine_table + rotate_half(head_block) * sine_table


def spin_back(grad_rotated, cosine_table, sine_table):
    return grad_rotated * cosine_table - rotate_half(grad_rotated * sine_table)


def visible(segment_row):
    places = jnp.arange(segment_row.shape[0], dtype=jnp.int32)
    return (segment_row[:, None] == segment_row[None, :]) & (places[None, :] <= places[:, None])


def score_block(query_low, key_low, allowed):
    scores = jnp.einsum(
        "bqkgd,bskd->bkgqs", query_low, key_low, preferred_element_type=F32
    ) * HEAD_DIM ** (-0.5)
    return jnp.where(allowed[:, None, None], scores, -1e30)


def mm(a, b):
    return jnp.dot(a, b, preferred_element_type=F32)


def mm_t(a, b):
    return lax.dot_general(a, b, (((1,), (1,)), ((), ())), preferred_element_type=F32)


def t_mm(a, b):
    return lax.dot_general(a, b, (((0,), (0,)), ((), ())), preferred_element_type=F32)


def swap_mates(block):
    route = [(i, i ^ 1) for i in range(lax.axis_size("fsdp"))]
    return lax.ppermute(block, "fsdp", route)


def spread_matrix():
    d = lax.broadcasted_iota(jnp.int32, (D, DP), 0)
    p = lax.broadcasted_iota(jnp.int32, (D, DP), 1)
    return ((p // 16 == d // 14) & (p % 16 == d % 14)).astype(BF)


def layer_forward(h, weights, smalls, tables, spread):
    gate_w, up_w, down_w, qkv_w, out_w = weights
    gain_one, gain_two, bias = smalls
    cos, sin, allowed = tables
    scale_one = lax.rsqrt(jnp.mean(h * h, axis=-1, keepdims=True) + norm_epsilon)
    n1 = mm((h * scale_one * gain_one).astype(BF), spread).astype(BF)
    qkv = mm(n1, qkv_w) + bias
    qkv = qkv.reshape(MICRO, SEQ, QKV)
    q = spin(qkv[..., :D].reshape(MICRO, SEQ, HEADS, HEAD_DIM), cos[:, :, None], sin[:, :, None])
    k = spin(
        qkv[..., D : D + 128].reshape(MICRO, SEQ, KV_HEADS, HEAD_DIM), cos[:, :, None], sin[:, :, None]
    )
    v = qkv[..., D + 128 :].reshape(MICRO, SEQ, KV_HEADS, HEAD_DIM).astype(BF)
    q = q.astype(BF).reshape(MICRO, SEQ, KV_HEADS, HEADS // KV_HEADS, HEAD_DIM)
    k = k.astype(BF)
    scores = score_block(q, k, allowed)
    row_max = jnp.max(scores, axis=-1, keepdims=True)
    exponent = jnp.exp(scores - row_max)
    row_total = jnp.sum(exponent, axis=-1, keepdims=True)
    probs = (exponent / row_total).astype(BF)
    lse = row_max + jnp.log(row_total)
    ctx = jnp.einsum("bkgqs,bskd->bqkgd", probs, v, preferred_element_type=F32)
    ctx = mm(ctx.reshape(MICRO * SEQ, D).astype(BF), spread).astype(BF)
    mid = h + mm(ctx, out_w)
    scale_two = lax.rsqrt(jnp.mean(mid * mid, axis=-1, keepdims=True) + norm_epsilon)
    n2 = mm((mid * scale_two * gain_two).astype(BF), spread).astype(BF)
    n2 = jnp.concatenate([n2, swap_mates(n2)], axis=0)
    gate = mm(n2, gate_w)
    up = mm(n2, up_w)
    act = (jax.nn.silu(gate) * up).astype(BF)
    part = mm(act, down_w)
    y = mid + part[: MICRO * SEQ] + swap_mates(part[MICRO * SEQ :].astype(BF)).astype(F32)
    return y, (h, scale_one, n1, q, k, v, lse, ctx, mid, scale_two, n2, gate, up, act)


def layer_backward(dy, kept, weights, smalls, tables, spread):
    h, scale_one, n1, q, k, v, lse, ctx, mid, scale_two, n2, gate, up, act = kept
    gate_w, up_w, down_w, qkv_w, out_w = weights
    gain_one, gain_two, bias = smalls
    cos, sin, allowed = tables
    dy_all = jnp.concatenate([dy, swap_mates(dy)], axis=0)
    dact = mm_t(dy_all, down_w)
    sig = jax.nn.sigmoid(gate)
    dgate = (dact * up * sig * (1.0 + gate * (1.0 - sig))).astype(BF)
    dup = (dact * gate * sig).astype(BF)
    part = mm_t(dgate, gate_w) + mm_t(dup, up_w)
    half = MICRO * SEQ
    dn2 = part[:half] + swap_mates(part[half:].astype(BF)).astype(F32)
    dn2 = mm_t(dn2.astype(BF), spread)
    g2 = jnp.sum(dn2 * mid * scale_two, axis=0)
    scaled = dn2 * gain_two
    dmid = (
        dy.astype(F32)
        + scale_two * scaled
        - mid * scale_two**3 * jnp.mean(scaled * mid, axis=-1, keepdims=True)
    )
    dbranch = dmid.astype(BF)
    dctx = mm_t(mm_t(dbranch, out_w).astype(BF), spread).astype(BF)
    dctx = dctx.reshape(MICRO, SEQ, KV_HEADS, HEADS // KV_HEADS, HEAD_DIM)
    scores = score_block(q, k, allowed)
    full = jnp.where(allowed[:, None, None], jnp.exp(scores - lse), 0.0)
    probs = full.astype(BF)
    dv = jnp.einsum("bkgqs,bqkgd->bskd", probs, dctx, preferred_element_type=F32)
    dprobs = jnp.einsum("bqkgd,bskd->bkgqs", dctx, v, preferred_element_type=F32)
    dscores = (full * (dprobs - jnp.sum(full * dprobs, axis=-1, keepdims=True))).astype(BF)
    dq = jnp.einsum("bkgqs,bskd->bqkgd", dscores, k, preferred_element_type=F32) * 0.125
    dk = jnp.einsum("bkgqs,bqkgd->bskd", dscores, q, preferred_element_type=F32) * 0.125
    dq = spin_back(dq.reshape(MICRO, SEQ, HEADS, HEAD_DIM), cos[:, :, None], sin[:, :, None])
    dk = spin_back(dk, cos[:, :, None], sin[:, :, None])
    dqkv = jnp.concatenate(
        [dq.reshape(half, -1), dk.reshape(half, -1), dv.reshape(half, -1)], axis=1
    ).astype(BF)
    dbias = jnp.sum(dqkv, axis=0, dtype=F32)
    dn1 = mm_t(mm_t(dqkv, qkv_w).astype(BF), spread)
    g1 = jnp.sum(dn1 * h * scale_one, axis=0)
    scaled = dn1 * gain_one
    dh = (
        dmid
        + scale_one * scaled
        - h * scale_one**3 * jnp.mean(scaled * h, axis=-1, keepdims=True)
    )

    def grads():
        dq_w = t_mm(n1, dqkv).astype(BF).reshape(64, 16, QKV)
        row = jnp.zeros((64, 1, QKV), BF)
        row = row.at[:, 0, 0:14].set(g1.reshape(64, 14).astype(BF))
        row = row.at[:, 0, 32:46].set(g2.reshape(64, 14).astype(BF))
        row = row.at[:, 0, 64:82].set(dbias.reshape(64, 18).astype(BF))
        dq_w = jnp.concatenate([dq_w[:, :14], row, dq_w[:, 15:]], axis=1)
        return (
            t_mm(n2, dgate).astype(BF),
            t_mm(n2, dup).astype(BF),
            t_mm(act, dy_all).astype(BF),
            dq_w,
            t_mm(ctx, dbranch).astype(BF),
        )

    return dh, grads


def pack_hidden(w):
    w = jnp.pad(w.reshape(14, 32, 2, 76), ((0, 2), (0, 0), (0, 0), (0, 4)))
    return w.transpose(2, 0, 1, 3).reshape(2, 16, 2560)


def unpack_hidden(g):
    g = g.reshape(2, 16, 32, 80)[:, :14, :, :76]
    return g.transpose(1, 2, 0, 3).reshape(14, 4864)


def hop(block, distance):
    route = [(0, 1)] if distance == 1 else [(1, 0)]
    return lax.ppermute(block, "section", route)


def shards(
    tokens_in, out_grad, segments, norm1_gain, qkv_weight, qkv_bias, out_weight, norm2_gain,
    gate_weight, up_weight, down_weight,
):
    section = lax.axis_index("section")
    half = MICRO * SEQ
    tokens = tokens_in.reshape(half, D)
    dy_last = out_grad.reshape(half, D)
    rows = segments[:, 0]
    cos, sin = jax.vmap(rope_tables, in_axes=(0, None))(rows, HEAD_DIM)
    tables = (cos, sin, jax.vmap(visible)(rows))
    spread = spread_matrix()
    small_row = jnp.concatenate(
        [jnp.pad(norm1_gain[0], (0, 18)), jnp.pad(norm2_gain[0], (0, 18)), jnp.pad(qkv_bias[0], (0, 1152 - 82))]
    )
    g, u, d, q, o = all_gather_weights(
        pack_hidden(gate_weight[0]),
        pack_hidden(up_weight[0]),
        jnp.pad(down_weight[0], ((0, 4), (0, 0))),
        jnp.concatenate([qkv_weight[0], small_row[None], jnp.zeros((1, QKV), BF)], axis=0),
        jnp.pad(out_weight[0], ((0, 2), (0, 0))),
    )
    weights = (
        g.reshape(DP, 2560), u.reshape(DP, 2560), d.reshape(2560, D), q.reshape(DP, QKV), o.reshape(DP, D)
    )
    small = q.reshape(64, 16, QKV)[:, 14, :128].astype(F32)
    smalls = (
        small[:, 0:14].reshape(1, D), small[:, 32:46].reshape(1, D), small[:, 64:82].reshape(1, QKV)
    )
    y, _ = layer_forward(tokens.astype(F32), weights, smalls, tables, spread)
    arrived = hop(y.astype(BF), 1)
    h = jnp.where(section == 0, tokens, arrived).astype(F32)
    y, kept = layer_forward(h, weights, smalls, tables, spread)
    dh, _ = layer_backward(dy_last, kept, weights, smalls, tables, spread)
    arrived = hop(dh.astype(BF), -1)
    dy = jnp.where(section == 1, dy_last, arrived)
    dh, grads = layer_backward(dy, kept, weights, smalls, tables, spread)
    parts = grads()
    shapes = bufs_shapes()
    g, u, d, q, o = reduce_scatter_grads(*[a.reshape(s) for a, s in zip(parts, shapes)])
    shape = (1, MICRO, 1, SEQ, D)
    return (
        y.astype(BF).reshape(shape),
        dh.astype(BF).reshape(shape),
        q[14, 0:14][None],
        q[:14][None],
        q[14, 64:82][None],
        o[:14][None],
        q[14, 32:46][None],
        unpack_hidden(g)[None],
        unpack_hidden(u)[None],
        d[:76][None],
    )


def solution(mesh):
    in_specs = (
        P(None, "fsdp", None, None),
        P(None, "fsdp", None, None),
        P(None, "fsdp", None),
        P("section", "fsdp"),
        P("section", "fsdp", None),
        P("section", "fsdp"),
        P("section", "fsdp", None),
        P("section", "fsdp"),
        P("section", "fsdp", None),
        P("section", "fsdp", None),
        P("section", "fsdp", None),
    )
    out_specs = (
        P("section", None, "fsdp", None, None),
        P("section", None, "fsdp", None, None),
        P("section", "fsdp"),
        P("section", "fsdp", None),
        P("section", "fsdp"),
        P("section", "fsdp", None),
        P("section", "fsdp"),
        P("section", "fsdp", None),
        P("section", "fsdp", None),
        P("section", "fsdp", None),
    )
    return jax.shard_map(shards, mesh=mesh, in_specs=in_specs, out_specs=out_specs, check_vma=False)
```

time: 1920 us -> 477 us (0.25)
  blocking collectives: 859 us -> 0 us
  waiting for transfers between devices: 472 us -> 27 us
  Pallas kernels: 0 us -> 210 us
  local copies, waits for them, and re-layouts: 253 us -> 49.2 us
  starting transfers between devices: 135 us -> 26 us
    unnamed x3 -> x0, blocking collectives: 717 us -> none
    all_gather x5 -> x0, waiting for transfers between devices: 411 us -> none  [the longest x1 122 us: shards(): lax.all_gather(gate_weight[0], 'fsdp', axis=0, tiled=True)]
    pallas_call x0 -> x2, Pallas kernels: none -> 210 us  [the longest x1 114 us: reduce_scatter_grads(): pl.pallas_call(rs_kernel, out_shape=[jax.ShapeDtypeStruct(s, F32) for s i...]
    unnamed x159 -> x115, local copies, waits for them, and re-layouts: 167 us -> 8.12 us
    all_gather x1 -> x0, blocking collectives: 143 us -> none  [shards(): lax.all_gather(norm1_gain[0], 'fsdp', axis=0, tiled=True)]
    unnamed x36 -> x0, starting transfers between devices: 123 us -> none
    another operation x43 -> x10, local copies, waits for them, and re-layouts: 44.5 us -> 7.86 us  [the longest x4 3.22 us: pack_hidden(): w = jnp.pad(w.reshape(14, 32, 2, 76), ((0, 2), (0, 0), (0, 0), (0, 4)))]
    ppermute x4 -> x10, waiting for transfers between devices: 51.1 us -> 27 us  [the longest x2 23.5 us: hop(): return lax.ppermute(block, 'section', route)]
  transfers between devices with their start and end apart: 45 -> 10, of which waited for: 11 -> 5; matrix products, arithmetic and copies ran while one was open for 17% -> 9% of each run, Pallas kernels for 0% -> 0%
where the time goes in v1:
time: 477 us; the launch traced here: 474 us
  Pallas kernels  210 us (44%)
  matrix products  131 us (27%)
  local copies, waits for them, and re-layouts  49.2 us (10%)
  other arithmetic  28.7 us (6%)
  waiting for transfers between devices  27 us (6%)
  starting transfers between devices  26 us (5%)
    pallas_call x1, Pallas kernels, reduce_scatter_grads(): pl.pallas_call(rs_kernel, out_shape=[jax.ShapeDtypeStruct(s, F32) for s i...  114 us
    pallas_call x1, Pallas kernels, all_gather_weights(): pl.pallas_call(ag_kernel, out_shape=[jax.ShapeDtypeStruct(s, BF) for s in...  95.9 us
    dot_general x12, matrix products, mm_t(): lax.dot_general(a, b, (((1,), (1,)), ((), ())), preferred_element_type=F32)  56.4 us
    dot_general x13, matrix products, mm(): return jnp.dot(a, b, preferred_element_type=F32)  45 us
    ppermute x2, waiting for transfers between devices, hop(): return lax.ppermute(block, 'section', route)  23.5 us
    ppermute x8, starting transfers between devices, swap_mates(): return lax.ppermute(block, 'fsdp', route)  20.2 us
    dot_general x5, matrix products, t_mm(): lax.dot_general(a, b, (((0,), (0,)), ((), ())), preferred_element_type=F32)  18 us
    reshape x4, local copies, waits for them, and re-layouts, layer_backward(): dctx = dctx.reshape(MICRO, SEQ, KV_HEADS, HEADS // KV_HEADS, HEAD_DIM)  10.5 us
  transfers between devices with their start and end apart: 10, of which 5 were waited for; matrix products, arithmetic and copies ran while one was open for 9% of the time, Pallas kernels for 0%

profile of v1, /device:TPU:1, one launch (start us, length us, event | category | flops | bytes accessed | tf_op | source)
XLA Modules:
  0.0 474.5 jit_solution(6607626572728955673)
XLA Ops:
  8.4 95.9 %gather_weights.1 = (bf16[4,2,4,32,2560]{4,3,2,1,0:T(8,128)(2,1)}, bf16[4,2,4,32,2560]{4,3,2,1,0:T(8,128)(2,1)}, bf16[4,2,4,80,896]{4,3,2,1,0:T(8,128)(2,1)}, bf...) custom-call(bf16[2,16,2560]{2,1,0:T(8,128)(2,1)} %reshape.442.g_in, bf16[2,16,2560]{2,1,0:T(8,128)(2,1)} %reshape.443.u_in, ...), custom_call_target="tpu_custom_call" | custom-call | tf_op jit(solution)/shard_map/gather_weights/pallas_call | solution.py:303
  107.3 4.5 convolution_add_fusion.1
  117.9 3.1 fusion.158
  124.2 3.3 multiply_reduce_fusion.4
  129.5 3.6 collective-permute-start
  134.6 7.7 %fusion.56 = f32[512,2560]{1,0:T(8,128)} fusion(bf16[1024,2560]{1,0:T(8,128)(2,1)} %bitcast.376, bf16[256,1024]{1,0:T(8,128)(2,1)S(1)} %collective-permute-done, bf16[256,1024]{1,0:T(8,128)(2,1)S(1)} %convolution_convert_fusion.12), kind=kOutput, calls=%fused_computation.148 | convolution fusion | flops 2686451712 | bytes 11534336 | tf_op jit(solution)/shard_map/dot_general | solution.py:597
  142.3 11.5 %fusion.5 = f32[512,896]{1,0:T(8,128)S(1)} fusion(bf16[2560,896]{1,0:T(8,128)(2,1)} %bitcast.388, f32[512,2560]{1,0:T(8,128)} %fusion.56, bf16[1024,2560]{1,0:T(8,128)(2,1)} %bitcast.382, bf16[256,1024]{1,0:T(8,128)(2,1)} %copy-done.42, bf16[256,1024]{1,0:T(8,128)(2,1)} %copy-done.41), kind=kOutput, calls=%fused_computation.21 | convolution fusion | flops 5043126272 | bytes 17956864 | tf_op jit(solution)/shard_map/dot_general | solution.py:597
  157.9 4.5 collective-permute-start.2
  163.2 9.1 %collective-permute-done.2 = bf16[256,896]{1,0:T(8,128)(2,1)S(1)} collective-permute-done((bf16[256,896]{1,0:T(8,128)(2,1)}, bf16[256,896]{1,0:T(8,128)(2,1)S(1)}, u32[]{:S(2)}, u32[]{:S(2)}) %collective-permute-start.2) | collective-permute-done | bytes 458784 | tf_op jit(solution)/shard_map/ppermute | solution.py:731
  180.4 13.2 %collective-permute-start.3 = (bf16[256,1024]{1,0:T(8,128)(2,1)S(1)}, bf16[256,1024]{1,0:T(8,128)(2,1)S(1)}, u32[]{:S(2)}, u32[]{:S(2)}) collective-permute-start(bf16[256,1024]{1,0:T(8,128)(2,1)S(1)} %convolution_convert_fusion.9), channel_id=1, source_target_pairs={{0,1},{1,0},{2,3},{3,2},{4,5},{5,4},{6,7},{7,6},{8,9},{9,8},{10,11... | collective-permute-start | bytes 1572872 | tf_op jit(solution)/shard_map/ppermute | solution.py:610
  193.6 6.0 %fusion.49 = f32[512,2560]{1,0:T(8,128)} fusion(bf16[2560,896]{1,0:T(8,128)(2,1)S(1)} %bitcast.392, bf16[256,896]{1,0:T(8,128)(2,1)} %collective-permute-done.5, bf16[256,896]{1,0:T(8,128)(2,1)} %bitcast.47), kind=kOutput, calls=%fused_computation.126 | convolution fusion | flops 2350645248 | bytes 10747904 | tf_op jit(solution)/shard_map/dot_general | solution.py:601
  199.7 4.6 fusion.154
  204.4 4.6 fusion.153
  209.0 7.4 %fusion.2 = f32[512,1024]{1,0:T(8,128)S(1)} fusion(bf16[1024,2560]{1,0:T(8,128)(2,1)S(1)} %bitcast.387, f32[512,2560]{1,0:T(8,128)} %fusion.49, f32[512,2560]{1,0:T(8,128)} %fusion.153, f32[512,2560]{1,0:T(8,128)} %fusion.154), kind=kOutput, calls=%fused_computation.18 | convolution fusion | flops 2697461760 | bytes 23068672 | tf_op jit(solution)/shard_map/dot_general | solution.py:601
  216.4 5.7 %fusion.14 = f32[512,1024]{1,0:T(8,128)S(1)} fusion(f32[512,1024]{1,0:T(8,128)S(1)} %fusion.2, bf16[1024,2560]{1,0:T(8,128)(2,1)S(1)} %bitcast.381, f32[512,2560]{1,0:T(8,128)} %fusion.49, f32[512,2560]{1,0:T(8,128)} %fusion.154), kind=kOutput, calls=%fused_computation.50 | convolution fusion | flops 2692743168 | bytes 19922944 | tf_op jit(solution)/shard_map/dot_general | solution.py:601
  227.3 4.1 convolution_convert_fusion.18
  233.9 2.7 copy.67
  246.1 4.6 fusion.35
  254.6 14.5 %collective-permute-done.7 = bf16[256,896]{1,0:T(8,128)(2,1)} collective-permute-done((bf16[256,896]{1,0:T(8,128)(2,1)}, bf16[256,896]{1,0:T(8,128)(2,1)}, u32[]{:S(2)}, u32[]{:S(2)}) %collective-permute-start.7) | collective-permute-done | bytes 458784 | tf_op jit(solution)/shard_map/ppermute | solution.py:731
  274.3 9.0 %multiply_convert_fusion = (bf16[512,2560]{1,0:T(8,128)(2,1)S(1)}, bf16[512,2560]{1,0:T(8,128)(2,1)S(1)}, bf16[512,2560]{1,0:T(8,128)(2,1)S(1)}) fusion(f32[512,2560]{1,0:T(8,128)} %fusion.154, f32[512,2560]{1,0:T(8,128)} %fusion.153, bf16[2560,896]{1,0:T(8,128)(2,1)} %bitcast.389, bf16[256,896]{1,0:T(8,128)(2,1)S(1)} %collective-permute-done.8, ...), kind=kOutput, calls=%fused_computation.4 | convolution fusion | flops 2371616768 | bytes 23855104 | tf_op jit(solution)/shard_map/dot_general | solution.py:601
  283.3 2.9 fusion.168
  286.3 4.9 %fusion.169 = f32[512,1024]{1,0:T(8,128)S(1)} fusion(bf16[512,2560]{1,0:T(8,128)(2,1)S(1)} %get-tuple-element.93, bf16[1024,2560]{1,0:T(8,128)(2,1)} %bitcast.383), kind=kOutput, calls=%fused_computation.293 | convolution fusion | flops 2684354560 | bytes 9961472 | tf_op jit(solution)/shard_map/dot_general | solution.py:601
  291.2 5.0 %convolution_add_fusion.2 = f32[512,1024]{1,0:T(8,128)S(1)} fusion(f32[512,1024]{1,0:T(8,128)S(1)} %fusion.169, bf16[512,2560]{1,0:T(8,128)(2,1)S(1)} %get-tuple-element.92, bf16[1024,2560]{1,0:T(8,128)(2,1)} %bitcast.377), kind=kOutput, calls=%fused_computation.51 | convolution fusion | flops 2684878848 | bytes 12058624 | tf_op jit(solution)/shard_map/dot_general | solution.py:601
  296.8 4.7 convolution_convert_fusion
  301.5 4.7 convolution_convert_fusion.1
  306.3 4.5 convolution_convert_fusion.2
  315.9 3.8 convolution_convert_fusion.17
  319.7 2.7 reshape.491
  322.4 2.7 copy.79
  332.3 4.2 fusion.38
  344.4 2.7 pad_maximum_fusion
  347.1 114.4 %scatter_grads.1 = (f32[2,16,2560]{2,1,0:T(8,128)}, f32[2,16,2560]{2,1,0:T(8,128)}, f32[80,896]{1,0:T(8,128)}, f32[16,1152]{1,0:T(8,128)}, f32[16,896]{1,0:T(8,128)}) custom-call(bf16[4,2,4,32,2560]{4,3,2,1,0:T(8,128)(2,1)} %bitcast.317, bf16[4,2,4,32,2560]{4,3,2,1,0:T(8,128)(2,1)} %bitcast.316, bf16[4,2,4,80,896]{4,3,2,1,0:T(8,128)(2,1)} %bitcast.318, ...), custom_call_target="tpu_custom_call" | custom-call | tf_op jit(solution)/shard_map/scatter_grads/pallas_call | solution.py:543
  (288 shorter events, 95.8 us)
Async XLA Ops:
  0.7 6.2 %copy-start.34 = (bf16[1,18]{1,0:T(2,128)(2,1)S(1)}, bf16[1,18]{1,0:T(2,128)(2,1)}, u32[]{:S(2)}) copy-start(bf16[1,18]{1,0:T(2,128)(2,1)} %param.22) | copy-start | bytes 112
  0.7 6.2 %copy-start.43 = (bf16[1,14]{1,0:T(2,128)(2,1)S(1)}, bf16[1,14]{1,0:T(2,128)(2,1)}, u32[]{:S(2)}) copy-start(bf16[1,14]{1,0:T(2,128)(2,1)} %param.20) | copy-start | bytes 88
  0.7 6.2 %copy-start.44 = (bf16[1,14]{1,0:T(2,128)(2,1)S(1)}, bf16[1,14]{1,0:T(2,128)(2,1)}, u32[]{:S(2)}) copy-start(bf16[1,14]{1,0:T(2,128)(2,1)} %param.24) | copy-start | bytes 88
  0.7 6.3 %copy-start.32 = (bf16[1,14,896]{2,1,0:T(8,128)(2,1)S(1)}, bf16[1,14,896]{2,1,0:T(8,128)(2,1)}, u32[]{:S(2)}) copy-start(bf16[1,14,896]{2,1,0:T(8,128)(2,1)} %param.23) | copy-start | bytes 75268
  0.7 7.0 %copy-start.31 = (bf16[1,14,1152]{2,1,0:T(8,128)(2,1)S(1)}, bf16[1,14,1152]{2,1,0:T(8,128)(2,1)}, u32[]{:S(2)}) copy-start(bf16[1,14,1152]{2,1,0:T(8,128)(2,1)} %param.21) | copy-start | bytes 96772
  2.4 103.3 %copy-start.17 = (bf16[2,1,128,896]{3,2,1,0:T(8,128)(2,1)S(1)}, bf16[2,1,128,896]{3,2,1,0:T(8,128)(2,1)}, u32[]{:S(2)}) copy-start(bf16[2,1,128,896]{3,2,1,0:T(8,128)(2,1)} %param.17) | copy-start | bytes 1376260
  107.3 69.6 %copy-start = (pred[896,1024]{1,0:T(32,128)(4,1)}, pred[896,1024]{1,0:T(32,128)(4,1)S(1)}, u32[]{:S(2)}) copy-start(pred[896,1024]{1,0:T(32,128)(4,1)S(1)} %fusion.1) | copy-start | bytes 2752516
  129.5 12.8 %copy-start.41 = (bf16[256,1024]{1,0:T(8,128)(2,1)}, bf16[256,1024]{1,0:T(8,128)(2,1)S(1)}, u32[]{:S(2)}) copy-start(bf16[256,1024]{1,0:T(8,128)(2,1)S(1)} %convolution_convert_fusion.12) | copy-start | bytes 1572868
  129.5 5.1 %collective-permute-start = (bf16[256,1024]{1,0:T(8,128)(2,1)S(1)}, bf16[256,1024]{1,0:T(8,128)(2,1)S(1)}, u32[]{:S(2)}, u32[]{:S(2)}) collective-permute-start(bf16[256,1024]{1,0:T(8,128)(2,1)S(1)} %convolution_convert_fusion.12), channel_id=1, source_target_pairs={{0,1},{1,0},{2,3},{3,2},{4,5},{5,4},{6,7},{7,6},{8,9},{9,8},{10,11... | collective-permute-start | bytes 1572872 | tf_op jit(solution)/shard_map/ppermute | solution.py:610
  134.6 7.7 %copy-start.42 = (bf16[256,1024]{1,0:T(8,128)(2,1)}, bf16[256,1024]{1,0:T(8,128)(2,1)S(1)}, u32[]{:S(2)}) copy-start(bf16[256,1024]{1,0:T(8,128)(2,1)S(1)} %collective-permute-done) | copy-start | bytes 1572868
  153.9 1.9 collective-permute-start.1
  157.9 14.4 %collective-permute-start.2 = (bf16[256,896]{1,0:T(8,128)(2,1)}, bf16[256,896]{1,0:T(8,128)(2,1)S(1)}, u32[]{:S(2)}, u32[]{:S(2)}) collective-permute-start(bf16[256,896]{1,0:T(8,128)(2,1)} %fusion.44), channel_id=1, source_target_pairs={{0,64},{1,65},{2,66},{3,67},{4,68},{5,69},{6,70},{7,71},{8,72},{9,... | collective-permute-start | bytes 1376264 | tf_op jit(solution)/shard_map/ppermute | solution.py:731
  162.4 31.2 %collective-permute-start.5 = (bf16[256,896]{1,0:T(8,128)(2,1)}, bf16[256,896]{1,0:T(8,128)(2,1)}, u32[]{:S(2)}, u32[]{:S(2)}) collective-permute-start(bf16[256,896]{1,0:T(8,128)(2,1)} %bitcast.47), channel_id=1, source_target_pairs={{0,1},{1,0},{2,3},{3,2},{4,5},{5,4},{6,7},{7,6},{8,9},{9,8},{10,11... | collective-permute-start | bytes 1376264 | tf_op jit(solution)/shard_map/ppermute | solution.py:610
  163.2 10.1 %copy-start.36 = (bf16[4,2,4,32,1152]{4,3,2,1,0:T(8,128)(2,1)S(1)}, bf16[4,2,4,32,1152]{4,3,2,1,0:T(8,128)(2,1)}, u32[]{:S(2)}) copy-start(bf16[4,2,4,32,1152]{4,3,2,1,0:T(8,128)(2,1)} %get-tuple-element.56) | copy-start | bytes 7077892
  175.2 18.5 %slice-start.4 = ((s8[4587520]{0:T(1024)(128)(4,1)}), s8[4194304]{0:T(1024)(128)(4,1)S(1)}, s32[]{:S(2)}) async-start(s8[4587520]{0:T(1024)(128)(4,1)} %bitcast.390), calls=%async_computation.4 | async-start | bytes 8388608
  176.0 17.7 %slice-start.5 = ((s8[4587520]{0:T(1024)(128)(4,1)}), s8[393216]{0:T(1024)(128)(4,1)S(1)}, s32[]{:S(2)}) async-start(s8[4587520]{0:T(1024)(128)(4,1)} %bitcast.390), calls=%async_computation.5 | async-start | bytes 786432
  179.6 20.1 %slice-start.2 = ((s8[5242880]{0:T(1024)(128)(4,1)}), s8[4194304]{0:T(1024)(128)(4,1)S(1)}, s32[]{:S(2)}) async-start(s8[5242880]{0:T(1024)(128)(4,1)} %bitcast.384), calls=%async_computation.2 | async-start | bytes 8388608
  180.4 24.0 %copy-start.37 = (bf16[256,1024]{1,0:T(8,128)(2,1)}, bf16[256,1024]{1,0:T(8,128)(2,1)S(1)}, u32[]{:S(2)}) copy-start(bf16[256,1024]{1,0:T(8,128)(2,1)S(1)} %convolution_convert_fusion.9) | copy-start | bytes 1572868
  180.4 19.3 %slice-start.3 = ((s8[5242880]{0:T(1024)(128)(4,1)}), s8[1048576]{0:T(1024)(128)(4,1)S(1)}, s32[]{:S(2)}) async-start(s8[5242880]{0:T(1024)(128)(4,1)} %bitcast.384), calls=%async_computation.3 | async-start | bytes 2097152
  180.4 19.3 %collective-permute-start.3 = (bf16[256,1024]{1,0:T(8,128)(2,1)S(1)}, bf16[256,1024]{1,0:T(8,128)(2,1)S(1)}, u32[]{:S(2)}, u32[]{:S(2)}) collective-permute-start(bf16[256,1024]{1,0:T(8,128)(2,1)S(1)} %convolution_convert_fusion.9), channel_id=1, source_target_pairs={{0,1},{1,0},{2,3},{3,2},{4,5},{5,4},{6,7},{7,6},{8,9},{9,8},{10,11... | collective-permute-start | bytes 1572872 | tf_op jit(solution)/shard_map/ppermute | solution.py:610
  193.6 10.7 %slice-start = ((s8[5242880]{0:T(1024)(128)(4,1)}), s8[4194304]{0:T(1024)(128)(4,1)S(1)}, s32[]{:S(2)}) async-start(s8[5242880]{0:T(1024)(128)(4,1)} %bitcast.378), calls=%async_computation | async-start | bytes 8388608
  222.2 2.0 collective-permute-start.6
  250.7 22.2 %copy-start.35 = (s32[3]{0:T(128)S(1)}, s32[3]{0:T(128)}, u32[]{:S(2)}) copy-start(s32[3]{0:T(128)} %constant.170.clone.1) | copy-start | bytes 40
  253.3 15.7 %collective-permute-start.7 = (bf16[256,896]{1,0:T(8,128)(2,1)}, bf16[256,896]{1,0:T(8,128)(2,1)}, u32[]{:S(2)}, u32[]{:S(2)}) collective-permute-start(bf16[256,896]{1,0:T(8,128)(2,1)} %fusion.27), channel_id=1, source_target_pairs={{64,0},{65,1},{66,2},{67,3},{68,4},{69,5},{70,6},{71,7},{72,8},{73... | collective-permute-start | bytes 1376264 | tf_op jit(solution)/shard_map/ppermute | solution.py:731
  270.3 4.0 collective-permute-start.8
  272.8 10.4 %slice-start.6 = ((s8[4587520]{0:T(1024)(128)(4,1)}), s8[393216]{0:T(1024)(128)(4,1)S(1)}, s32[]{:S(2)}) async-start(s8[4587520]{0:T(1024)(128)(4,1)} %bitcast.393), calls=%async_computation.6 | async-start | bytes 786432
  274.3 9.0 %slice-start.7 = ((s8[4587520]{0:T(1024)(128)(4,1)}), s8[4194304]{0:T(1024)(128)(4,1)S(1)}, s32[]{:S(2)}) async-start(s8[4587520]{0:T(1024)(128)(4,1)} %bitcast.393), calls=%async_computation.7 | async-start | bytes 8388608
  286.2 25.6 %collective-permute-start.4 = (bf16[256,896]{1,0:T(8,128)(2,1)S(1)}, bf16[256,896]{1,0:T(8,128)(2,1)S(1)}, u32[]{:S(2)}, u32[]{:S(2)}) collective-permute-start(bf16[256,896]{1,0:T(8,128)(2,1)S(1)} %slice.348), channel_id=1, source_target_pairs={{0,1},{1,0},{2,3},{3,2},{4,5},{5,4},{6,7},{7,6},{8,9},{9,8},{10,11... | collective-permute-start | bytes 1376264 | tf_op jit(solution)/shard_map/ppermute | solution.py:610
  291.2 5.6 %copy-start.38 = (bf16[256,1024]{1,0:T(8,128)(2,1)S(1)}, bf16[256,1024]{1,0:T(8,128)(2,1)}, u32[]{:S(2)}) copy-start(bf16[256,1024]{1,0:T(8,128)(2,1)} %copy-done.37) | copy-start | bytes 1572868
  291.2 5.6 %copy-start.40 = (bf16[256,1024]{1,0:T(8,128)(2,1)S(1)}, bf16[256,1024]{1,0:T(8,128)(2,1)}, u32[]{:S(2)}) copy-start(bf16[256,1024]{1,0:T(8,128)(2,1)} %copy-done.39) | copy-start | bytes 1572868
  296.2 14.5 %collective-permute-start.9 = (bf16[256,1024]{1,0:T(8,128)(2,1)S(1)}, bf16[256,1024]{1,0:T(8,128)(2,1)S(1)}, u32[]{:S(2)}, u32[]{:S(2)}) collective-permute-start(bf16[256,1024]{1,0:T(8,128)(2,1)S(1)} %slice.346), channel_id=1, source_target_pairs={{0,1},{1,0},{2,3},{3,2},{4,5},{5,4},{6,7},{7,6},{8,9},{9,8},{10,11... | collective-permute-start | bytes 1572872 | tf_op jit(solution)/shard_map/ppermute | solution.py:610
  461.5 6.9 %copy-start.26 = (f32[2,16,2560]{2,1,0:T(8,128)S(1)}, f32[2,16,2560]{2,1,0:T(8,128)}, u32[]{:S(2)}) copy-start(f32[2,16,2560]{2,1,0:T(8,128)} %get-tuple-element.64) | copy-start | bytes 983044
  (31 other events, 77.9 us)

commit v2 on v1

v2 whole, which is shorter than its diff:
```python
import math
from types import SimpleNamespace

import jax
import jax.numpy as jnp
from jax import lax
from jax.experimental import pallas as pl
from jax.experimental.pallas import tpu as pltpu
from jax.sharding import PartitionSpec as P
import numpy as np

HEADS = 14
KV_HEADS = 2
HEAD_DIM = 64
MICRO = 2
SEQ = 128
D = 896
DP = 1024
QKV = 1152
norm_epsilon = 1e-06
rope_base = 1000000.0

MESH = pl.DeviceIdType.MESH
BF = jnp.bfloat16
F32 = jnp.float32


class Place:
    def __init__(self):
        f = lax.axis_index("fsdp")
        self.s = lax.axis_index("section")
        self.c = lax.rem(f, 2)
        self.z = lax.rem(f // 2, 4)
        self.y = lax.rem(f // 8, 2)
        self.x = f // 16

    def at(self, x=None, y=None, z=None, c=None):
        x = self.x if x is None else x
        y = self.y if y is None else y
        z = self.z if z is None else z
        c = self.c if c is None else c
        return (self.s, ((x * 2 + y) * 4 + z) * 2 + c)

    def step(self, axis, k):
        here = self.x if axis == "x" else self.z
        return lax.rem(here + (k + 4), 4)

    def to(self, axis, k):
        return self.at(**{axis: self.step(axis, k)})

    def across(self):
        return self.at(y=1 - self.y)

    def mate(self):
        return self.at(c=1 - self.c)

    def beyond(self):
        return (1 - self.s, self.at()[1])


def greet(place):
    barrier = pltpu.get_barrier_semaphore()
    near = (
        place.to("x", 1), place.to("x", -1), place.to("z", 1), place.to("z", -1),
        place.across(), place.mate(), place.beyond(),
    )
    for device in near:
        pl.semaphore_signal(barrier, inc=1, device_id=device, device_id_type=MESH)
    pl.semaphore_wait(barrier, len(near))


class Wire:
    def __init__(self, send_sems, recv_sems):
        self.send_sems, self.recv_sems = send_sems, recv_sems
        self.count, self.started = 0, []

    def send(self, src, dst, device):
        k = self.count
        self.count += 1
        assert k < self.send_sems.shape[0]
        copy = pltpu.make_async_remote_copy(
            src_ref=src, dst_ref=dst, send_sem=self.send_sems.at[k],
            recv_sem=self.recv_sems.at[k], device_id=device, device_id_type=MESH,
        )
        copy.start()
        self.started.append(copy)
        return copy

    def drain(self):
        for copy in self.started:
            copy.wait_send()
        self.started = []


def interleave(flows):
    waiting = [(next(flow), k, flow) for k, flow in enumerate(flows)]
    while waiting:
        waiting.sort(key=lambda item: item[:2])
        _, k, flow = waiting.pop(0)
        try:
            waiting.append((next(flow), k, flow))
        except StopIteration:
            pass


def gather_yab(wire, place, slot, first, last, ready, t0, unit):
    x, y, z = place.x, place.y, place.z
    yield t0
    for wait in ready:
        wait()
    cross = wire.send(slot(x, y, z), slot(x, y, z), place.across())

    def pos(a, b):
        return (b, a) if first == "z" else (a, b)

    def piece(a, b, half=None):
        px, pz = pos(a, b)
        return slot(px, half, pz)

    mine = {"x": x, "z": z}
    a0, b0 = mine[first], mine[last]
    t = t0 + unit * 1
    yield t
    cross.wait_recv()
    a_r = wire.send(piece(a0, b0), piece(a0, b0), place.to(first, 1))
    a_l = wire.send(piece(a0, b0), piece(a0, b0), place.to(first, -1))

    def last_sends(a):
        r = wire.send(piece(a, b0), piece(a, b0), place.to(last, 1))
        l = wire.send(piece(a, b0), piece(a, b0), place.to(last, -1))
        return r, l

    def last_forward(a, r, l):
        r.wait_recv()
        bm = place.step(last, -1)
        r2 = wire.send(piece(a, bm, 0), piece(a, bm, 0), place.to(last, 1))
        l.wait_recv()
        bp = place.step(last, 1)
        l2 = wire.send(piece(a, bp, 1), piece(a, bp, 1), place.to(last, -1))
        return r2, l2

    w0 = last_sends(a0)
    t += unit * 2
    yield t
    a_r.wait_recv()
    am = place.step(first, -1)
    a_r2 = wire.send(piece(am, b0, 0), piece(am, b0, 0), place.to(first, 1))
    a_l.wait_recv()
    ap = place.step(first, 1)
    a_l2 = wire.send(piece(ap, b0, 1), piece(ap, b0, 1), place.to(first, -1))
    w1 = last_sends(am)
    w2 = last_sends(ap)
    t += unit * 2
    yield t
    f0 = last_forward(a0, *w0)
    t += unit * 2
    yield t
    a_r2.wait_recv()
    a_l2.wait_recv()
    aq = place.step(first, 2)
    w3 = last_sends(aq)
    t += unit * 2
    yield t
    f1 = last_forward(am, *w1)
    t += unit * 2
    yield t
    f2 = last_forward(ap, *w2)
    t += unit * 2
    yield t
    f3 = last_forward(aq, *w3)
    t += unit * 2
    yield t
    for pair in (f0, f1, f2, f3):
        for copy in pair:
            copy.wait_recv()


def gather_aby(wire, place, slot, parts, t0, unit):
    x, y, z = place.x, place.y, place.z
    yield t0
    r = wire.send(slot(x, y, z), slot(x, y, z), place.to("x", 1))
    l = wire.send(slot(x, y, z), slot(x, y, z), place.to("x", -1))
    t = t0 + unit
    yield t
    r.wait_recv()
    xm, xp = place.step("x", -1), place.step("x", 1)
    r2 = wire.send(parts(xm, y, z, 0), parts(xm, y, z, 0), place.to("x", 1))
    l.wait_recv()
    l2 = wire.send(parts(xp, y, z, 1), parts(xp, y, z, 1), place.to("x", -1))
    t += unit
    yield t
    r2.wait_recv()
    l2.wait_recv()
    zr = wire.send(slot(None, y, z), slot(None, y, z), place.to("z", 1))
    zl = wire.send(slot(None, y, z), slot(None, y, z), place.to("z", -1))
    y0 = wire.send(slot(None, y, z), slot(None, y, z), place.across())
    t += unit * 4
    yield t
    zm, zp, zq = place.step("z", -1), place.step("z", 1), place.step("z", 2)
    zr.wait_recv()
    zr2 = wire.send(slot(0, y, zm), slot(0, y, zm), place.to("z", 1))
    y1 = wire.send(slot(None, y, zm), slot(None, y, zm), place.across())
    zl.wait_recv()
    zl2 = wire.send(slot(1, y, zp), slot(1, y, zp), place.to("z", -1))
    y2 = wire.send(slot(None, y, zp), slot(None, y, zp), place.across())
    t += unit * 4
    yield t
    zr2.wait_recv()
    zl2.wait_recv()
    y3 = wire.send(slot(None, y, zq), slot(None, y, zq), place.across())
    t += unit * 10
    yield t
    for copy in (y0, y1, y2, y3):
        copy.wait_recv()


BLOCK = dict(G=(32, 2560), U=(32, 2560), D=(80, 896), Q=(32, 1152), O=(32, 896))


def gather_flows(wire, place, ins, bufs, local_sems, done):
    x, y, z, c = place.x, place.y, place.z, place.c
    rows = pl.ds(pl.multiple_of(c * 16, 16), 16)
    G, U, D, Q, O = bufs
    g_in, u_in, d_in, q_in, o_in = ins
    own = []
    for k, (src, dst) in enumerate((
        (g_in.at[c], G.at[x, y, z, rows]), (u_in.at[c], U.at[x, y, z, rows]),
        (d_in, D.at[x, y, z]), (q_in, Q.at[x, y, z, rows]), (o_in, O.at[x, y, z, rows]),
    )):
        copy = pltpu.make_async_copy(src, dst, local_sems.at[k])
        copy.start()
        own.append(copy)
    swap_g = wire.send(g_in.at[1 - c], G.at[x, y, z, rows], place.mate())
    swap_u = wire.send(u_in.at[1 - c], U.at[x, y, z, rows], place.mate())

    def whole(buf):
        def slot(px, half, pz):
            if half is None:
                return buf.at[px, :, pz]
            return buf.at[px, half, pz]
        return slot

    def part(buf):
        def slot(px, half, pz):
            if half is None:
                return buf.at[px, :, pz, rows]
            return buf.at[px, half, pz, rows]
        return slot

    def down_slot(px, py, pz):
        if px is None:
            return D.at[:, py, pz]
        return D.at[px, py, pz]

    def down_zslot(px, py, pz):
        if px is None:
            return D.at[:, py, pz]
        if isinstance(px, int):
            return D.at[pl.ds(2 * px, 2), py, pz]
        return D.at[px, py, pz]

    def down_parts(px, py, pz, half):
        r = pl.ds(0, 48) if half == 0 else pl.ds(48, 32)
        return D.at[px, py, pz, r]

    def attention(name, buf, k, t0):
        yield from gather_yab(wire, place, part(buf), "z", "x", (own[k].wait,), t0, 1.0)
        mine = buf.at[:, :, :, rows]
        swap = wire.send(mine, mine, place.mate())
        yield t0 + 20.0
        swap.wait_recv()
        done.add(name)

    def down(t0):
        yield t0
        own[2].wait()
        yield from gather_aby(wire, place, down_zslot, down_parts, t0, 2.0)

    flows = [
        attention("Q", Q, 3, 0.0),
        attention("O", O, 4, 0.1),
        down(0.2),
        gather_yab(wire, place, whole(G), "z", "x", (own[0].wait, swap_g.wait_recv), 0.3, 4.0),
        gather_yab(wire, place, whole(U), "x", "z", (own[1].wait, swap_u.wait_recv), 0.4, 4.0),
    ]
    return flows


def bufs_shapes():
    return [(4, 2, 4) + BLOCK[k] for k in "GUDQO"]


def add(dst, *srcs):
    total = dst[...]
    for src in srcs:
        total = total + src[...]
    dst[...] = total


def add_each(count, dst, *srcs):
    def body(i, carry):
        add(dst(i), *[src(i) for src in srcs])
        return carry
    lax.fori_loop(0, count, body, 0)


def scatter_aby(wire, place, slot, R, first, last, t0, unit):
    r1a, r1b, r2a, r2b, s1a, s1b, s2a, s2b, t_buf = R
    mine = {"x": place.x, "z": place.z}
    a0, b0 = mine[first], mine[last]

    def piece(a, b, half=None):
        return slot(b, half, a) if first == "z" else slot(a, half, b)

    def blocks(a, b):
        return lambda i: piece(a, b, i)

    ap, am, aq = place.step(first, 1), place.step(first, -1), place.step(first, 2)
    order = [place.step(last, k) for k in (2, 1, -1)] + [b0]
    t = t0
    yield t
    one = []
    for k, b in enumerate(order):
        one.append((
            wire.send(piece(aq, b, 0), r1a.at[k], place.to(first, 1)),
            wire.send(piece(aq, b, 1), r1b.at[k], place.to(first, -1)),
        ))
    two = []
    for k, b in enumerate(order):
        t = t0 + unit * (k + 1)
        yield t
        one[k][0].wait_recv()
        add(piece(ap, b, 0), r1a.at[k])
        right = wire.send(piece(ap, b), r2a.at[k], place.to(first, 1))
        one[k][1].wait_recv()
        add(piece(am, b, 1), r1b.at[k])
        left = wire.send(piece(am, b), r2b.at[k], place.to(first, -1))
        two.append((right, left))
    t1 = t0 + unit * 4
    bp, bm, bq = order[1], order[2], order[0]

    def settle(k):
        two[k][0].wait_recv()
        two[k][1].wait_recv()
        for i in range(2):
            add(piece(a0, order[k], i), r2a.at[k, i], r2b.at[k, i])

    yield t1 + 2 * unit
    settle(0)
    d_r = wire.send(piece(a0, bq, 0), s1a, place.to(last, 1))
    d_l = wire.send(piece(a0, bq, 1), s1b, place.to(last, -1))
    yield t1 + 4 * unit
    settle(1)
    d_r.wait_recv()
    add(piece(a0, bp, 0), s1a)
    e_r = wire.send(piece(a0, bp), s2a, place.to(last, 1))
    yield t1 + 6 * unit
    settle(2)
    d_l.wait_recv()
    add(piece(a0, bm, 1), s1b)
    e_l = wire.send(piece(a0, bm), s2b, place.to(last, -1))
    yield t1 + 8 * unit
    settle(3)
    yield t1 + 9 * unit
    e_r.wait_recv()
    e_l.wait_recv()
    for i in range(2):
        add(piece(a0, b0, i), s2a.at[i], s2b.at[i])
    other = slot(place.x, 1 - place.y, place.z)
    cross = wire.send(other, t_buf, place.across())
    yield t1 + 10 * unit
    cross.wait_recv()
    add(slot(place.x, place.y, place.z), t_buf)


def scatter_down(wire, place, D, R, t0, unit):
    yb, z1a, z1b, z2a, z2b, xa, xb, x2a, x2b = R
    x, y, z = place.x, place.y, place.z
    zp, zm, zq = place.step("z", 1), place.step("z", -1), place.step("z", 2)
    xp, xm, xq = place.step("x", 1), place.step("x", -1), place.step("x", 2)
    top, low = pl.ds(0, 48), pl.ds(48, 32)
    lo, hi = pl.ds(0, 2), pl.ds(2, 2)
    order = (zq, zp, zm, z)
    yield t0
    crossing = [wire.send(D.at[:, 1 - y, b], yb.at[k], place.across()) for k, b in enumerate(order)]

    def settle(k):
        crossing[k].wait_recv()
        add_each(4, lambda i: D.at[i, y, order[k]], lambda i: yb.at[k, i])

    yield t0 + 3 * unit
    settle(0)
    d_r = wire.send(D.at[lo, y, zq], z1a, place.to("z", 1))
    d_l = wire.send(D.at[hi, y, zq], z1b, place.to("z", -1))
    yield t0 + 6 * unit
    settle(1)
    d_r.wait_recv()
    add_each(2, lambda i: D.at[i, y, zp], lambda i: z1a.at[i])
    e_r = wire.send(D.at[:, y, zp], z2a, place.to("z", 1))
    yield t0 + 9 * unit
    settle(2)
    d_l.wait_recv()
    add_each(2, lambda i: D.at[i + 2, y, zm], lambda i: z1b.at[i])
    e_l = wire.send(D.at[:, y, zm], z2b, place.to("z", -1))
    yield t0 + 12 * unit
    settle(3)
    yield t0 + 13 * unit
    e_r.wait_recv()
    e_l.wait_recv()
    add_each(4, lambda i: D.at[i, y, z], lambda i: z2a.at[i], lambda i: z2b.at[i])
    f_r = wire.send(D.at[xq, y, z, top], xa, place.to("x", 1))
    f_l = wire.send(D.at[xq, y, z, low], xb, place.to("x", -1))
    yield t0 + 14 * unit
    f_r.wait_recv()
    add(D.at[xp, y, z, top], xa)
    g_r = wire.send(D.at[xp, y, z], x2a, place.to("x", 1))
    f_l.wait_recv()
    add(D.at[xm, y, z, low], xb)
    g_l = wire.send(D.at[xm, y, z], x2b, place.to("x", -1))
    yield t0 + 15 * unit
    g_r.wait_recv()
    g_l.wait_recv()
    add(D.at[x, y, z], x2a, x2b)


def rs_scratch():
    def aby(rows, cols):
        shapes = [(4, rows, cols)] * 2 + [(4, 2, rows, cols)] * 2 + [(rows, cols)] * 2 + [(2, rows, cols)] * 2 + [(rows, cols)]
        return [pltpu.VMEM(s, BF) for s in shapes]
    out = []
    out += aby(32, 2560) + [pltpu.VMEM((16, 2560), BF)]
    out += aby(32, 2560) + [pltpu.VMEM((16, 2560), BF)]
    b = (80, 896)
    out += [pltpu.VMEM(s, BF) for s in (
        (4, 4) + b, (2,) + b, (2,) + b, (4,) + b, (4,) + b, (48, 896), (32, 896), b, b)]
    out += aby(16, 1152) + [pltpu.VMEM((4, 2, 4, 16, 1152), BF)]
    out += aby(16, 896) + [pltpu.VMEM((4, 2, 4, 16, 896), BF)]
    return out


N_RS_SCRATCH = 10 + 10 + 9 + 10 + 10


def scatter_flows(wire, place, bufs, R, made, outs):
    x, y, z, c = place.x, place.y, place.z, place.c
    G, U, D, Q, O = bufs
    g_o, u_o, d_o, q_o, o_o = outs
    rg, ru, rd, rq, ro = R[:10], R[10:20], R[20:29], R[29:39], R[39:49]
    rows = pl.ds(pl.multiple_of(c * 16, 16), 16)
    others = pl.ds(pl.multiple_of(16 - c * 16, 16), 16)

    def whole(buf):
        def slot(px, half, pz):
            return buf.at[px, :, pz] if half is None else buf.at[px, half, pz]
        return slot

    def part(buf):
        def slot(px, half, pz):
            return buf.at[px, :, pz, rows] if half is None else buf.at[px, half, pz, rows]
        return slot

    def made_of(name):
        t = 0.0
        while name not in made:
            yield t
            t += 0.5
        return t

    def hidden(name, buf, out, r, first, last):
        t0 = yield from made_of(name)
        yield from scatter_aby(wire, place, whole(buf), r[:9], first, last, t0, 4.0)
        swap = wire.send(buf.at[x, y, z, others], r[9], place.mate())
        yield 200.0
        swap.wait_recv()
        out[c] = buf[x, y, z, rows].astype(F32)
        out[1 - c] = r[9][...].astype(F32)

    def attention(name, buf, out, r):
        t0 = yield from made_of(name)
        swap = wire.send(buf.at[:, :, :, others], r[9], place.mate())
        yield t0 + 8.0
        swap.wait_recv()
        add_each(32, lambda i: buf.at[i // 8, lax.rem(i // 4, 2), lax.rem(i, 4), rows],
                 lambda i: r[9].at[i // 8, lax.rem(i // 4, 2), lax.rem(i, 4)])
        yield from scatter_aby(wire, place, part(buf), r[:9], "x", "z", t0 + 8.0, 1.0)
        out[...] = buf[x, y, z, rows].astype(F32)

    def down():
        t0 = yield from made_of("D")
        yield from scatter_down(wire, place, D, rd, t0, 4.0)
        d_o[...] = D[x, y, z].astype(F32)

    return [
        down(),
        hidden("G", G, g_o, rg, "x", "z"),
        hidden("U", U, u_o, ru, "z", "x"),
        attention("O", O, o_o, ro),
        attention("Q", Q, q_o, rq),
    ]


TOK = 256
FF = 2560


def mm(a, b):
    return jnp.dot(a, b, preferred_element_type=F32)


def mm_t(a, b):
    return lax.dot_general(a, b, (((1,), (1,)), ((), ())), preferred_element_type=F32)


def t_mm(a, b):
    return lax.dot_general(a, b, (((0,), (0,)), ((), ())), preferred_element_type=F32)


def constants():
    d = np.arange(D)
    spread = np.zeros((D, DP), np.float32)
    spread[d, 16 * (d // 14) + d % 14] = 1
    pick = np.zeros((64, DP), np.float32)
    pick[np.arange(64), 16 * np.arange(64) + 14] = 1
    own14 = (np.arange(64)[:, None] == d[None] // 14).astype(np.float32)
    j = np.arange(QKV)
    own18 = (np.arange(64)[:, None] == j[None] // 18).astype(np.float32)
    lane = np.arange(128)[:, None]
    e1 = (lane == d[None] % 14).astype(np.float32)
    e2 = (lane == 32 + d[None] % 14).astype(np.float32)
    eb = (lane == 64 + j[None] % 18).astype(np.float32)
    return [jnp.asarray(a, BF) for a in (spread, pick, own14, own18, e1, e2, eb)]


CONST = ("spread", "pick", "own14", "own18", "e1", "e2", "eb")


def cols(buf, start, size):
    value = buf[:, :, :, :, pl.ds(start, size)]
    return value.reshape(-1, size)


def put(ref, value):
    ref[...] = value.reshape(ref.shape)


def rotate(x, lo32):
    return jnp.where(lo32, pltpu.roll(x, 96, 1), pltpu.roll(x, 32, 1))


def lane_is(shape, width, below):
    lane = lax.broadcasted_iota(jnp.int32, shape, 1)
    return lax.rem(lane, width) < below


def gains(R):
    q = cols(R.Q, 0, 128)
    s = mm(R.pick[...], q).astype(BF)
    R.g1[...] = jnp.sum(mm(s, R.e1[...]) * R.own14[...].astype(F32), axis=0, keepdims=True)
    R.g2[...] = jnp.sum(mm(s, R.e2[...]) * R.own14[...].astype(F32), axis=0, keepdims=True)
    R.bias[...] = jnp.sum(mm(s, R.eb[...]) * R.own18[...].astype(F32), axis=0, keepdims=True)


def inverse_rms(h):
    return lax.rsqrt(jnp.sum(h * h, axis=-1, keepdims=True) * (1.0 / D) + norm_epsilon)


def project_qkv(R, source):
    h = source[...].astype(F32)
    n1 = (h * inverse_rms(h) * R.g1[...]).astype(BF)
    R.N1[...] = mm(n1, R.spread[...]).astype(BF)
    lo32 = lane_is((TOK, 128), 64, 32)
    cos, sin = R.cos[...], R.sin[...]
    for start, size in ((0, 256), (256, 256), (512, 256), (768, 256), (1024, 128)):
        out = mm(R.N1[...], cols(R.Q, start, size)) + R.bias[:, start:start + size]
        for k in range(size // 128):
            x = out[:, 128 * k:128 * k + 128]
            tile = (start + 128 * k) // 128
            if tile < 8:
                x = x * cos + rotate(x, lo32) * sin
            if tile < 7:
                R.QR[:, 128 * tile:128 * tile + 128] = x.astype(BF)
            else:
                x = x.astype(BF).astype(F32)
                swapped = pltpu.roll(x, 64, 1)
                lo = lane_is((TOK, 128), 128, 64)
                R.KV[tile - 7, 0] = jnp.where(lo, x, swapped).astype(BF)
                R.KV[tile - 7, 1] = x.astype(BF)
                R.KV[tile - 7, 2] = jnp.where(lo, swapped, x).astype(BF)


def two_heads(R, tile):
    return jnp.concatenate([tile * R.lanes[0], tile * R.lanes[1]], axis=0)


def beside(x):
    return jnp.concatenate([x[:SEQ], x[SEQ:]], axis=1)


def tile_at(t):
    return pl.ds(pl.multiple_of(t * 128, 128), 128)


def variant_of(t):
    return jnp.where(t < 3, 0, jnp.where(t > 3, 2, 1))


def probs_of(R, b, t, rows):
    q2 = two_heads(R, R.QR[rows, tile_at(t)])
    kk = R.KV[0, variant_of(t), rows]
    mask = R.mask[b]
    s = mm_t(q2, kk) * 0.125 + jnp.concatenate([mask, mask], axis=0)
    e = jnp.exp(s - jnp.max(s, axis=-1, keepdims=True))
    p = e / jnp.sum(e, axis=-1, keepdims=True)
    return q2, kk, p


def attend(R, b):
    rows = pl.ds(b * SEQ, SEQ)

    def body(t, carry):
        _, _, p = probs_of(R, b, t, rows)
        vv = two_heads(R, R.KV[1, variant_of(t), rows])
        R.DQKV[rows, tile_at(t)] = mm(beside(p.astype(BF)), vv).astype(BF)
        return carry

    lax.fori_loop(0, 7, body, 0)


def after_attention(R, source):
    R.CP[...] = mm(R.DQKV[:, :D], R.spread[...]).astype(BF)
    mid = source[...].astype(F32) + mm(R.CP[...], cols(R.O, 0, D))
    R.MID[...] = mid
    n2 = (mid * inverse_rms(mid) * R.g2[...]).astype(BF)
    R.N2[0:TOK] = mm(n2, R.spread[...]).astype(BF)


def exchange(R, k, src, dst, device):
    return pltpu.make_async_remote_copy(
        src_ref=src, dst_ref=dst, send_sem=R.xs.at[k], recv_sem=R.xr.at[k],
        device_id=device, device_id_type=MESH,
    )


def hidden(R, rows):
    def body(j, carry):
        at = pl.ds(pl.multiple_of(j * 256, 256), 256)
        n2 = R.N2[rows]
        gate = mm(n2, R.G[:, :, :, :, at].reshape(DP, 256))
        up = mm(n2, R.U[:, :, :, :, at].reshape(DP, 256))
        R.GA[rows, at] = gate.astype(BF)
        R.UP[rows, at] = up.astype(BF)
        R.ACT[rows, at] = (gate / (1.0 + jnp.exp(-gate)) * up).astype(BF)
        return carry

    lax.fori_loop(0, FF // 256, body, 0)


def feed_forward(R, place):
    own, other = pl.ds(0, TOK), pl.ds(TOK, TOK)
    n2 = exchange(R, 0, R.N2.at[own], R.N2.at[other], place.mate())
    n2.start()
    hidden(R, own)
    n2.wait_recv()
    hidden(R, other)
    down = R.D[...].reshape(FF, D)
    R.DB[...] = mm(R.ACT[other], down).astype(BF)
    part = exchange(R, 1, R.DB, R.DC, place.mate())
    part.start()
    y = R.MID[...] + mm(R.ACT[own], R.D[...].reshape(FF, D))
    part.wait_recv()
    R.y[...] = (y + R.DC[...].astype(F32)).astype(BF)
    n2.wait_send()
    part.wait_send()


def hidden_back(R, rows, acc):
    acc[...] = jnp.zeros_like(acc)

    def body(j, carry):
        at = pl.ds(pl.multiple_of(j * 640, 640), 640)
        down = R.D[j].reshape(640, D)
        for start, size in ((0, 256), (256, 256), (512, 128)):
            sub = pl.ds(pl.multiple_of(j * 640 + start, 128), size)
            dact = mm_t(R.DY[rows], down[start:start + size])
            gate = R.GA[rows, sub].astype(F32)
            up = R.UP[rows, sub].astype(F32)
            sig = 1.0 / (1.0 + jnp.exp(-gate))
            R.GA[rows, sub] = (dact * up * sig * (1.0 + gate * (1.0 - sig))).astype(BF)
            R.UP[rows, sub] = (dact * gate * sig).astype(BF)
        acc[...] += mm_t(R.GA[rows, at], R.G[:, :, :, :, at].reshape(DP, 640))
        acc[...] += mm_t(R.UP[rows, at], R.U[:, :, :, :, at].reshape(DP, 640))
        return carry

    lax.fori_loop(0, FF // 640, body, 0)


def attend_back(R, b):
    rows = pl.ds(b * SEQ, SEQ)
    R.dkv[...] = jnp.zeros_like(R.dkv)
    cos, sin = R.cos[rows], R.sin[rows]
    lo32 = lane_is((SEQ, 128), 64, 32)

    def spin_back(g):
        return g * cos + rotate(g * sin, lo32)

    def body(t, carry):
        q2, kk, p = probs_of(R, b, t, rows)
        var = variant_of(t)
        dc2 = two_heads(R, R.DC[rows, tile_at(t)])
        dp = mm_t(dc2, R.KV[1, var, rows])
        ds = (p * (dp - jnp.sum(p * dp, axis=-1, keepdims=True))).astype(BF)
        R.dkv[0, var] += t_mm(ds, q2)
        R.dkv[1, var] += t_mm(p.astype(BF), dc2)
        dq = mm(beside(ds), two_heads(R, kk)) * 0.125
        R.DQKV[rows, tile_at(t)] = spin_back(dq).astype(BF)
        return carry

    lax.fori_loop(0, 7, body, 0)
    lo = lane_is((SEQ, 128), 128, 64)

    def joined(k):
        first, mixed, last = R.dkv[k, 0], R.dkv[k, 1], R.dkv[k, 2]
        return mixed + jnp.where(
            lo, first + pltpu.roll(first, 64, 1), last + pltpu.roll(last, 64, 1)
        )

    R.DQKV[rows, 896:1024] = spin_back(joined(0) * 0.125).astype(BF)
    R.DQKV[rows, 1024:1152] = joined(1).astype(BF)


def backward(R, place):
    own, other = pl.ds(0, TOK), pl.ds(TOK, TOK)
    dy = exchange(R, 3, R.DY.at[own], R.DY.at[other], place.mate())
    dy.start()
    dy.wait_recv()
    hidden_back(R, other, R.acc)
    R.dn[...] = R.acc[...].astype(BF)
    dn = exchange(R, 4, R.dn, R.dn_in, place.mate())
    dn.start()
    hidden_back(R, own, R.acc)
    dn.wait_recv()
    dn2p = (R.acc[...] + R.dn_in[...].astype(F32)).astype(BF)
    dn2 = mm_t(dn2p, R.spread[...])
    mid = R.MID[...]
    inv2 = inverse_rms(mid)
    R.dg2[...] = jnp.sum(dn2 * mid * inv2, axis=0, keepdims=True)
    scaled = dn2 * R.g2[...]
    mean = jnp.sum(scaled * mid, axis=-1, keepdims=True) * (1.0 / D)
    dmid = R.DY[own].astype(F32) + inv2 * scaled - mid * (inv2 * inv2 * inv2 * mean)
    R.MID[...] = dmid
    R.DB[...] = dmid.astype(BF)
    dctx = mm_t(R.DB[...], cols(R.O, 0, D)).astype(BF)
    R.DC[...] = mm_t(dctx, R.spread[...]).astype(BF)
    attend_back(R, 0)
    attend_back(R, 1)
    dqkv = R.DQKV[...]
    R.dbias[...] = jnp.sum(dqkv.astype(F32), axis=0, keepdims=True)
    dn1 = mm_t(mm_t(dqkv, cols(R.Q, 0, QKV)).astype(BF), R.spread[...])
    h = R.h[...].astype(F32)
    inv1 = inverse_rms(h)
    R.dg1[...] = jnp.sum(dn1 * h * inv1, axis=0, keepdims=True)
    scaled = dn1 * R.g1[...]
    mean = jnp.sum(scaled * h, axis=-1, keepdims=True) * (1.0 / D)
    R.dh[...] = (R.MID[...] + inv1 * scaled - h * (inv1 * inv1 * inv1 * mean)).astype(BF)
    dy.wait_send()
    dn.wait_send()


def weight_grads(R, done, t):
    def down(x, carry):
        at = pl.ds(pl.multiple_of(x * 640, 640), 640)
        for start, size in ((0, 512), (512, 384)):
            grad = t_mm(R.ACT[:, at], R.DY[:, start:start + size])
            put(R.D.at[x, :, :, :, pl.ds(start, size)], grad.astype(BF))
        return carry

    yield t
    lax.fori_loop(0, 4, down, 0)
    done.add("D")
    for name, buf, grad in (("G", R.G, R.GA), ("U", R.U, R.UP)):
        def tile(x, carry):
            n2 = R.N2[:, pl.ds(pl.multiple_of(x * 256, 256), 256)]
            for start in range(0, FF, 512):
                at = pl.ds(start, 512)
                put(buf.at[x, :, :, :, at], t_mm(n2, grad[:, at]).astype(BF))
            return carry

        t += 3.0
        yield t
        lax.fori_loop(0, 4, tile, 0)
        done.add(name)
    t += 3.0
    yield t

    def out_rows(x, carry):
        rows = pl.ds(pl.multiple_of(x * 256, 256), 256)
        put(R.O.at[x], t_mm(R.CP[:, rows], R.DB[...]).astype(BF))
        return carry

    lax.fori_loop(0, 4, out_rows, 0)
    done.add("O")
    t += 1.0
    yield t
    small = (
        mm_t((R.own14[...].astype(F32) * R.dg1[...]).astype(BF), R.e1[...])
        + mm_t((R.own14[...].astype(F32) * R.dg2[...]).astype(BF), R.e2[...])
        + mm_t((R.own18[...].astype(F32) * R.dbias[...]).astype(BF), R.eb[...])
    )
    R.small[...] = small.astype(BF)

    def qkv_rows(x, carry):
        rows = pl.ds(pl.multiple_of(x * 256, 256), 256)
        n1 = R.N1[:, rows]
        for start in range(0, QKV, 384):
            g = t_mm(n1, R.DQKV[:, start:start + 384])
            if start == 0:
                g = jnp.concatenate([g[:, :128] + t_mm(R.pick[:, rows], R.small[...]), g[:, 128:]], axis=1)
            put(R.Q.at[x, :, :, :, pl.ds(start, 384)], g.astype(BF))
        return carry

    lax.fori_loop(0, 4, qkv_rows, 0)
    done.add("Q")


INS = ("g_in", "u_in", "d_in", "q_in", "o_in", "tokens", "og", "cos", "sin", "mask") + CONST
OUTS = ("y", "dh", "g_o", "u_o", "d_o", "q_o", "o_o")
LOCAL = (
    ("h", (TOK, D), BF), ("N1", (TOK, DP), BF), ("QR", (TOK, D), BF),
    ("KV", (2, 3, TOK, 128), BF), ("CP", (TOK, DP), BF),
    ("MID", (TOK, D), F32), ("N2", (2 * TOK, DP), BF), ("GA", (2 * TOK, FF), BF),
    ("UP", (2 * TOK, FF), BF), ("ACT", (2 * TOK, FF), BF), ("DY", (2 * TOK, D), BF), ("acc", (TOK, DP), F32), ("dn", (TOK, DP), BF), ("dn_in", (TOK, DP), BF),
    ("DB", (TOK, D), BF), ("DC", (TOK, D), BF), ("DQKV", (TOK, QKV), BF),
    ("dkv", (2, 3, SEQ, 128), F32), ("lanes", (2, SEQ, 128), BF),
    ("small", (64, 128), BF),
    ("g1", (1, D), F32), ("g2", (1, D), F32), ("bias", (1, QKV), F32),
    ("dg1", (1, D), F32), ("dg2", (1, D), F32), ("dbias", (1, QKV), F32),
)


def layers_kernel(*refs):
    names = INS + OUTS + tuple("GUDQO") + tuple(name for name, _, _ in LOCAL)
    R = SimpleNamespace(**dict(zip(names, refs)))
    rest = refs[len(names):]
    land = rest[:N_RS_SCRATCH]
    R.ss, R.rs, R.ls, R.xs, R.xr = rest[N_RS_SCRATCH:]
    place = Place()
    first = place.s == 0
    greet(place)
    wire = Wire(R.ss, R.rs)
    bufs = (R.G, R.U, R.D, R.Q, R.O)
    done = set()

    def early():
        lo = lane_is((SEQ, 128), 128, 64).astype(F32)
        R.lanes[0] = lo.astype(BF)
        R.lanes[1] = (1.0 - lo).astype(BF)
        t = 20.0
        while not {"Q", "O"} <= done:
            yield t
            t += 1.0
        gains(R)
        project_qkv(R, R.tokens)
        t += 5.0
        yield t
        attend(R, 0)
        t += 5.0
        yield t
        attend(R, 1)
        t += 5.0
        yield t
        after_attention(R, R.tokens)

    @pl.when(first)
    def _():
        R.h[...] = R.tokens[...]

    ins = (R.g_in, R.u_in, R.d_in, R.q_in, R.o_in)
    interleave(gather_flows(wire, place, ins, bufs, R.ls, done) + [early()])

    hop_h = exchange(R, 2, R.y, R.h, place.beyond())
    hop_dy = exchange(R, 5, R.dh, R.DY.at[pl.ds(0, TOK)], place.beyond())

    @pl.when(place.s == 1)
    def _():
        R.DY[0:TOK] = R.og[...]
        hop_h.wait_recv()
        project_qkv(R, R.h)
        attend(R, 0)
        attend(R, 1)
        after_attention(R, R.h)

    feed_forward(R, place)

    @pl.when(first)
    def _():
        hop_h.start()
        hop_dy.wait_recv()

    backward(R, place)

    @pl.when(place.s == 1)
    def _():
        hop_dy.start()

    wire.drain()
    outs = (R.g_o, R.u_o, R.d_o, R.q_o, R.o_o)
    made = set()
    flows = scatter_flows(wire, place, bufs, land, made, outs)
    interleave([weight_grads(R, made, 0.0)] + flows)
    wire.drain()

    @pl.when(first)
    def _():
        hop_h.wait_send()

    @pl.when(place.s == 1)
    def _():
        hop_dy.wait_send()


N_WIRE = 208


def run_layers(ins):
    outs = [(TOK, D), (TOK, D), (2, 16, 2560), (2, 16, 2560), (80, 896), (16, 1152), (16, 896)]
    kinds = [BF, BF] + [F32] * 5
    vmem = pl.BlockSpec(memory_space=pltpu.VMEM)
    dma = pltpu.SemaphoreType.DMA
    return pl.pallas_call(
        layers_kernel,
        out_shape=[jax.ShapeDtypeStruct(s, k) for s, k in zip(outs, kinds)],
        in_specs=[vmem] * len(INS),
        out_specs=[vmem] * len(OUTS),
        scratch_shapes=[pltpu.VMEM(s, BF) for s in bufs_shapes()]
        + [pltpu.VMEM(s, k) for _, s, k in LOCAL]
        + rs_scratch()
        + [dma((N_WIRE,)), dma((N_WIRE,)), dma((5,)), dma((6,)), dma((6,))],
        compiler_params=pltpu.CompilerParams(
            collective_id=0, has_side_effects=True, vmem_limit_bytes=63 * 2**20
        ),
        name="two_layers",
    )(*ins)


def rope_tables(segment_row, head_size):
    length = segment_row.shape[0]
    places = jnp.arange(length, dtype=jnp.int32)
    changes = jnp.concatenate(
        [jnp.ones((1,), jnp.int32), (segment_row[1:] != segment_row[:-1]).astype(jnp.int32)]
    )
    starts = lax.cummax(places * changes, axis=0)
    offsets = (places - starts).astype(F32)
    ladder = jnp.arange(head_size // 2, dtype=F32) * (-2.0 * math.log(rope_base) / head_size)
    angles = offsets[:, None] * jnp.exp(ladder)[None, :]
    cos, sin = jnp.cos(angles), jnp.sin(angles)
    return (
        jnp.concatenate([cos, cos, cos, cos], axis=-1),
        jnp.concatenate([-sin, sin, -sin, sin], axis=-1),
    )


def mask_of(segment_row):
    places = jnp.arange(segment_row.shape[0], dtype=jnp.int32)
    seen = (segment_row[:, None] == segment_row[None, :]) & (places[None, :] <= places[:, None])
    return jnp.where(seen, 0.0, -1e30).astype(F32)


def pack_hidden(w):
    w = jnp.pad(w.reshape(14, 32, 2, 76), ((0, 2), (0, 0), (0, 0), (0, 4)))
    return w.transpose(2, 0, 1, 3).reshape(2, 16, 2560)


def unpack_hidden(g):
    g = g.reshape(2, 16, 32, 80)[:, :14, :, :76]
    return g.transpose(1, 2, 0, 3).reshape(14, 4864)


def shards(
    tokens_in, out_grad, segments, norm1_gain, qkv_weight, qkv_bias, out_weight, norm2_gain,
    gate_weight, up_weight, down_weight,
):
    half = MICRO * SEQ
    rows = segments[:, 0]
    cos, sin = jax.vmap(rope_tables, in_axes=(0, None))(rows, HEAD_DIM)
    small_row = jnp.concatenate(
        [jnp.pad(norm1_gain[0], (0, 18)), jnp.pad(norm2_gain[0], (0, 18)), jnp.pad(qkv_bias[0], (0, 1152 - 82))]
    )
    y, dh, g, u, d, q, o = run_layers([
        pack_hidden(gate_weight[0]),
        pack_hidden(up_weight[0]),
        jnp.pad(down_weight[0], ((0, 4), (0, 0))),
        jnp.concatenate([qkv_weight[0], small_row[None], jnp.zeros((1, QKV), BF)], axis=0),
        jnp.pad(out_weight[0], ((0, 2), (0, 0))),
        tokens_in.reshape(half, D),
        out_grad.reshape(half, D),
        cos.reshape(half, 128),
        sin.reshape(half, 128),
        jax.vmap(mask_of)(rows),
        *constants(),
    ])
    shape = (1, MICRO, 1, SEQ, D)
    return (
        y.reshape(shape),
        dh.reshape(shape),
        q[14, 0:14][None],
        q[:14][None],
        q[14, 64:82][None],
        o[:14][None],
        q[14, 32:46][None],
        unpack_hidden(g)[None],
        unpack_hidden(u)[None],
        d[:76][None],
    )


def solution(mesh):
    in_specs = (
        P(None, "fsdp", None, None),
        P(None, "fsdp", None, None),
        P(None, "fsdp", None),
        P("section", "fsdp"),
        P("section", "fsdp", None),
        P("section", "fsdp"),
        P("section", "fsdp", None),
        P("section", "fsdp"),
        P("section", "fsdp", None),
        P("section", "fsdp", None),
        P("section", "fsdp", None),
    )
    out_specs = (
        P("section", None, "fsdp", None, None),
        P("section", None, "fsdp", None, None),
        P("section", "fsdp"),
        P("section", "fsdp", None),
        P("section", "fsdp"),
        P("section", "fsdp", None),
        P("section", "fsdp"),
        P("section", "fsdp", None),
        P("section", "fsdp", None),
        P("section", "fsdp", None),
    )
    return jax.shard_map(shards, mesh=mesh, in_specs=in_specs, out_specs=out_specs, check_vma=False)
```

time: 477 us -> 364 us (0.76)
  matrix products: 131 us -> 0 us
  Pallas kernels: 210 us -> 334 us
  waiting for transfers between devices: 27 us -> 0 us
  starting transfers between devices: 26 us -> 0 us
  local copies, waits for them, and re-layouts: 49.2 us -> 23.5 us
  other arithmetic: 28.7 us -> 5.7 us
    dot_general x41 -> x0, matrix products: 128 us -> none  [the longest x12 56.4 us: mm_t(): lax.dot_general(a, b, (((1,), (1,)), ((), ())), preferred_element_type=F32)]
    pallas_call x2 -> x1, Pallas kernels: 210 us -> 334 us  [run_layers(): pl.pallas_call(layers_kernel, out_shape=[jax.ShapeDtypeStruct(s, k) for s...]
    ppermute x10 -> x0, waiting for transfers between devices: 27 us -> none  [the longest x2 23.5 us: hop(): return lax.ppermute(block, 'section', route)]
    ppermute x10 -> x0, starting transfers between devices: 26 us -> none  [the longest x8 20.2 us: swap_mates(): return lax.ppermute(block, 'fsdp', route)]
    reshape x4 -> x0, local copies, waits for them, and re-layouts: 10.5 us -> none  [layer_backward(): dctx = dctx.reshape(MICRO, SEQ, KV_HEADS, HEADS // KV_HEADS, HEAD_DIM)]
    convert_element_type x8 -> x0, other arithmetic: 7.06 us -> none  [the longest x1 2.64 us: shards(): arrived = hop(dh.astype(BF), -1)]
    another operation x9 -> x0, other arithmetic: 5.54 us -> none
    slice x18 -> x0, local copies, waits for them, and re-layouts: 5.22 us -> none  [the longest x2 1.3 us: layer_forward(): qkv[..., :D].reshape(MICRO, SEQ, HEADS, HEAD_DIM)]
  transfers between devices with their start and end apart: 10 -> 0, of which waited for: 5 -> 0; matrix products, arithmetic and copies ran while one was open for 9% -> 0% of each run, Pallas kernels for 0% -> 0%
where the time goes in v2:
time: 364 us
  Pallas kernels  334 us (92%)
  local copies, waits for them, and re-layouts  23.5 us (6%)
  other arithmetic  5.7 us (2%)
    pallas_call x1, Pallas kernels, run_layers(): pl.pallas_call(layers_kernel, out_shape=[jax.ShapeDtypeStruct(s, k) for s...  334 us

profile of v2, /device:TPU:1, one launch (start us, length us, event | category | flops | bytes accessed | tf_op | source)
XLA Modules:
  0.0 363.8 jit_solution(9791259195838126863)
XLA Ops:
  0.7 0.8 slice_compare_fusion
  1.6 0.7 pad.31
  2.2 0.7 pad.32
  3.0 0.7 pad.33
  3.7 1.4 pad.34.refs_4_
  5.1 1.5 maximum_maximum_fusion.refs_3_
  6.6 1.5 and_select_fusion.refs_9_
  8.2 0.2 reduce_window_max.15
  8.5 1.6 pad.30.refs_2_
  10.1 1.6 reshape_squeeze.6
  11.8 1.0 reshape.99.refs_0_
  12.8 0.7 reshape_squeeze.7
  13.6 1.0 reshape.100.refs_1_
  14.6 0.5 fusion
  15.1 1.0 pad_maximum_fusion
  16.1 333.8 %two_layers.1 = (bf16[256,896]{1,0:T(8,128)(2,1)}, bf16[256,896]{1,0:T(8,128)(2,1)}, f32[2,16,2560]{2,1,0:T(8,128)}, f32[2,16,2560]{2,1,0:T(8,128)}, f32[80,896]...) custom-call(bf16[2,16,2560]{2,1,0:T(8,128)(2,1)} %reshape.99.refs_0_, bf16[2,16,2560]{2,1,0:T(8,128)(2,1)} %reshape.100.refs_1_, ...), custom_call_target="tpu_custom_call" | custom-call | tf_op jit(solution)/shard_map/two_layers/pallas_call | solution.py:929
  349.9 1.3 slice.34
  351.2 1.3 fusion.3
  352.5 0.9 slice_bitcast_fusion.3
  353.4 0.7 copy.56
  354.1 0.8 slice_bitcast_fusion.4
  354.9 0.7 copy.57
  355.6 1.0 slice_bitcast_fusion.2
  356.6 1.0 copy.58
  357.6 0.3 reshape.105
  357.9 0.4 copy.52
  358.2 1.7 broadcast_in_dim_reshape.6
  359.9 0.3 reshape.106
  360.2 0.4 copy.53
  360.6 1.7 broadcast_in_dim_reshape.7
  362.3 0.8 copy.61
  363.0 0.8 copy.62
  (25 shorter events, 0.8 us)
Async XLA Ops:
  0.6 12.2 %copy-start.4 = (bf16[1,14,4864]{2,1,0:T(8,128)(2,1)S(1)}, bf16[1,14,4864]{2,1,0:T(8,128)(2,1)}, u32[]{:S(2)}) copy-start(bf16[1,14,4864]{2,1,0:T(8,128)(2,1)} %param.27) | copy-start | bytes 408580
  349.9 7.7 %copy-start.3 = (f32[2,16,2560]{2,1,0:T(8,128)S(1)}, f32[2,16,2560]{2,1,0:T(8,128)}, u32[]{:S(2)}) copy-start(f32[2,16,2560]{2,1,0:T(8,128)} %get-tuple-element.21) | copy-start | bytes 983044
  357.6 2.3 copy-start.2
  359.9 2.4 copy-start.1
  360.2 2.9 copy-start
